TPU v7x, 512 devices: a whole 4x4x16 slice. The times are simulated.
512 devices in a mesh: replica: 16 (over z_hi, y, core), fsdp: 32 (over x, z_lo).
Axes of the slice: x: 4, y: 4, z: 16 (z_hi: 2, z_lo: 8; z = z_hi * 8 + z_lo), core: 2. Of those that a mesh axis runs over, the one named last changes fastest.
Arguments:
- local_weights: bfloat16 [16, 2048, 512], P('replica', 'fsdp'), may hold values from -0.125 to 0.125
- global_weights: bfloat16 [2048, 512], P('fsdp'), may hold values from -0.125 to 0.125
- momentum: float32 [2048, 512], P('fsdp', 'replica'), may hold values from -0.12 to 0.12
- activations: bfloat16 [16, 8192, 2048], P('replica', 'fsdp'), may hold values from -6 to 6
- kv_cotangent: bfloat16 [16, 8192, 512], P('replica', 'fsdp'), may hold values from -6 to 6
Outputs:
- kv_rows: bfloat16 [16, 8192, 512], P('replica', 'fsdp')
- input_grad: bfloat16 [16, 8192, 2048], P('replica', 'fsdp')
- weight_grad: bfloat16 [16, 2048, 512], P('replica', 'fsdp')
- new_global: bfloat16 [2048, 512], P('fsdp')
- new_momentum: float32 [2048, 512], P('fsdp', 'replica')
All inputs are finite; a program needn't handle non-finite values. Where the computation divides by a largest or mean magnitude, that divisor is 1e-20 or more.
Results may differ from a plain program's by a relative error of at most 0.0038.
Values may be sent and summed in bfloat16 or wider, within the bound.
A program may use at most 64 MiB of HBM per device.

v0:
```python
import jax
import jax.numpy as jnp
from jax import lax
from jax.sharding import PartitionSpec as P

BLOCK = 64


outer_rate = 0.7
outer_momentum = 0.9
scale_epsilon = 1e-06


def per_device(local_weights, global_weights, momentum, activations, kv_cotangent):
    local_shard = local_weights[0]
    inputs_here = activations[0]
    cotangent = kv_cotangent[0]
    rows_here = local_shard.shape[0]
    kv_width = local_shard.shape[1]
    tok_rows = inputs_here.shape[0]
    token_weight = 1.0 / (tok_rows * lax.axis_size("fsdp"))
    columns = inputs_here
    kv_sum = jnp.dot(
        columns,
        lax.all_gather(local_shard, "fsdp", axis=0, tiled=True),
        preferred_element_type=jnp.float32,
    )
    grad_in = lax.dot_general(
        cotangent,
        lax.all_gather(local_shard, "fsdp", axis=0, tiled=True),
        (((1,), (1,)), ((), ())),
        preferred_element_type=jnp.float32,
    )
    columns = inputs_here
    grad_rows = lax.psum_scatter(
        lax.dot_general(
            columns, cotangent, (((0,), (0,)), ((), ())), preferred_element_type=jnp.float32
        )
        * token_weight,
        "fsdp",
        scatter_dimension=0,
        tiled=True,
    )
    replicas = lax.axis_size("replica")
    share_cols = kv_width // replicas
    block_count = kv_width // BLOCK
    my_replica = lax.axis_index("replica")
    drift = global_weights.astype(jnp.float32) - local_shard.astype(jnp.float32)
    drift_blocks = drift.reshape(rows_here, block_count, BLOCK)
    block_scale = (jnp.max(jnp.abs(drift_blocks), axis=2) + scale_epsilon).astype(jnp.bfloat16)
    quantized = (drift_blocks / block_scale.astype(jnp.float32)[..., None]).astype(jnp.bfloat16)
    unit_cols = min(BLOCK, share_cols)
    scale_units = jnp.repeat(block_scale, BLOCK // unit_cols, axis=1)
    units_share = share_cols // unit_cols
    quant_send = (
        quantized.reshape(rows_here, replicas, share_cols)
        .transpose(1, 0, 2)
        .reshape(replicas, rows_here * share_cols)
    )
    scale_send = (
        scale_units.reshape(rows_here, replicas, units_share)
        .transpose(1, 0, 2)
        .reshape(replicas, rows_here * units_share)
    )
    quant_got, scale_got = (
        lax.all_to_all(quant_send, "replica", split_axis=0, concat_axis=0, tiled=True),
        lax.all_to_all(scale_send, "replica", split_axis=0, concat_axis=0, tiled=True),
    )
    dequantized = (
        quant_got.reshape(replicas, rows_here, units_share, unit_cols).astype(jnp.float32)
        * scale_got.reshape(replicas, rows_here, units_share).astype(jnp.float32)[..., None]
    )
    mean_grad = jnp.sum(dequantized, axis=0).reshape(rows_here, share_cols) / replicas
    old_share = lax.dynamic_slice_in_dim(
        global_weights, my_replica * share_cols, share_cols, 1
    ).astype(jnp.float32)
    new_momentum = outer_momentum * momentum + mean_grad
    new_share = (old_share - outer_rate * (mean_grad + outer_momentum * new_momentum)).astype(
        jnp.bfloat16
    )
    new_global = lax.all_gather(new_share, "replica", axis=1, tiled=True)
    return (
        kv_sum.astype(jnp.bfloat16)[None],
        grad_in.astype(jnp.bfloat16)[None],
        grad_rows.astype(jnp.bfloat16)[None],
        new_global,
        new_momentum,
    )


def solution(mesh):
    placed = (
        P("replica", "fsdp", None),
        P("fsdp", None),
        P("fsdp", "replica"),
        P("replica", "fsdp", None),
        P("replica", "fsdp", None),
    )
    return jax.shard_map(
        per_device,
        mesh=mesh,
        in_specs=placed,
        out_specs=(
            P("replica", "fsdp", None),
            P("replica", "fsdp", None),
            P("replica", "fsdp", None),
            P("fsdp", None),
            P("fsdp", "replica"),
        ),
        check_vma=False,
    )
```

profile of v0, /device:TPU:8, one launch (start us, length us, event | category | flops | bytes accessed | tf_op | source)
XLA Modules:
  0.0 507.3 jit_solution(14764548510699401208)
XLA Ops:
  7.2 0.7 all-gather.3.cloned.1.call-update
  8.0 0.4 copy-done
  8.4 3.6 convolution_multiply_fusion
  12.1 0.8 copy-done.3
  12.9 0.1 copy.28
  13.0 0.1 copy.27
  13.1 0.1 bitcast_reduce_fusion
  13.2 0.6 copy.32
  13.8 18.2 %all-to-all-start.1 = ((bf16[16,1,64]{2,1,0:T(2,128)(2,1)}), bf16[16,1,64]{2,1,0:T(2,128)(2,1)S(1)}, u32[]{:S(2)}, u32[]{:S(2)}) async-start(bf16[16,1,64]{2,1,0:T(2,128)(2,1)} %copy.32), calls=%async_computation.2 | async-start | bytes 16384 | tf_op jit(solution)/shard_map/all_to_all | solution.py:67
  32.1 0.2 copy.29
  32.3 0.2 all_to_all.16
  32.5 0.5 broadcast.25
  33.0 1.0 reduce.5
  34.0 0.7 reshape.71
  34.6 10.7 %all-to-all-done.1 = bf16[16,1,64]{2,1,0:T(2,128)(2,1)S(1)} async-done(((bf16[16,1,64]{2,1,0:T(2,128)(2,1)}), bf16[16,1,64]{2,1,0:T(2,128)(2,1)S(1)}, u32[]{:S(2)}, u32[]{:S(2)}) %all-to-all-start.1) | async-done | bytes 2080 | tf_op jit(solution)/shard_map/all_to_all | solution.py:67
  45.3 4.8 all-to-all-start
  50.1 0.1 copy.33
  50.2 0.2 mul.41
  50.4 0.2 mul.42
  50.6 13.1 %all-to-all-done = bf16[16,2,1024]{2,1,0:T(2,128)(2,1)S(1)} async-done(((bf16[16,2,1024]{2,1,0:T(2,128)(2,1)}), bf16[16,2,1024]{2,1,0:T(2,128)(2,1)S(1)}, u32[]{:S(2)}, u32[]{:S(2)}) %all-to-all-start) | async-done | bytes 65568 | tf_op jit(solution)/shard_map/all_to_all | solution.py:66
  63.8 0.1 multiply_reduce_fusion
  63.8 0.1 div.27
  63.9 0.1 multiply_add_fusion
  64.0 0.1 copy.34
  64.1 35.3 %all_gather.8 = bf16[64,512]{0,1:T(8,128)(2,1)S(1)} all-gather(bf16[64,32]{0,1:T(8,128)(2,1)S(1)} %copy.34), channel_id=1, replica_groups=mesh['replica'=16,'fsdp'=32] {'replica'}, dimensions={1}, use_global_device_ids=true | all-gather | bytes 69632 | tf_op jit(solution)/shard_map/all_gather | solution.py:81
  99.4 0.7 copy.35
  100.1 0.7 copy.36
  100.8 140.2 %all-gather.3.cloned.1.call-done = bf16[1,2048,512]{2,1,0:T(8,128)(2,1)} async-done(((bf16[1,64,512]{2,1,0:T(8,128)(2,1)}), bf16[1,2048,512]{2,1,0:T(8,128)(2,1)}) %all-gather.3.cloned.1.call-update) | async-done | bytes 2097168 | tf_op jit(solution)/shard_map/all_gather | solution.py:25
  241.0 3.5 fusion
  244.4 1.4 fusion.7
  245.9 253.0 %reduce-scatter.2.cloned.1.call-done = f32[64,512]{1,0:T(8,128)} async-done(((f32[2048,512]{1,0:T(8,128)}), f32[64,512]{1,0:T(8,128)}) %reduce-scatter.2.cloned.1.call-update) | async-done | bytes 131088 | tf_op jit(solution)/shard_map/reduce_scatter | solution.py:35
  498.9 1.5 convert_bitcast_fusion
  (21 shorter events, 0.3 us)
Async XLA Ops:
  7.2 1.2 copy-start
  7.2 233.8 %all-gather.3.cloned.1.call-start = ((), (), s32[]{:S(2)}) async-start(), calls=%async_computation.4 | async-start | bytes 2162688 | tf_op jit(solution)/shard_map/all_gather | solution.py:25
  7.9 491.0 %reduce-scatter.2.cloned.1.call-start = ((), (), s32[]{:S(2)}) async-start(), calls=%async_computation.3 | async-start | bytes 4325376 | tf_op jit(solution)/shard_map/reduce_scatter | solution.py:35
  12.0 0.8 copy-start.3
  12.0 1.0 copy-start.4
  12.9 37.2 %copy-start.5 = (f32[64,32]{0,1:T(8,128)S(1)}, f32[64,32]{0,1:T(8,128)}, u32[]{:S(2)}) copy-start(f32[64,32]{0,1:T(8,128)} %param.7) | copy-start | bytes 24580
  13.8 31.5 %all-to-all-start.1 = ((bf16[16,1,64]{2,1,0:T(2,128)(2,1)}), bf16[16,1,64]{2,1,0:T(2,128)(2,1)S(1)}, u32[]{:S(2)}, u32[]{:S(2)}) async-start(bf16[16,1,64]{2,1,0:T(2,128)(2,1)} %copy.32), calls=%async_computation.2 | async-start | bytes 16384 | tf_op jit(solution)/shard_map/all_to_all | solution.py:67
  32.0 208.9 %copy-start.2 = (bf16[1,256,512]{2,1,0:T(8,128)(2,1)S(1)}, bf16[1,256,512]{2,1,0:T(8,128)(2,1)}, u32[]{:S(2)}) copy-start(bf16[1,256,512]{2,1,0:T(8,128)(2,1)} %param.9) | copy-start | bytes 786436
  45.3 18.4 %all-to-all-start = ((bf16[16,2,1024]{2,1,0:T(2,128)(2,1)}), bf16[16,2,1024]{2,1,0:T(2,128)(2,1)S(1)}, u32[]{:S(2)}, u32[]{:S(2)}) async-start(bf16[16,2,1024]{2,1,0:T(2,128)(2,1)} %reshape.71), calls=%async_computation.1 | async-start | bytes 131072 | tf_op jit(solution)/shard_map/all_to_all | solution.py:66
  241.0 3.5 copy-start.1
Sparse Core Ops, SparseCore 0:
  10.1 230.8 all-gather.2
  243.8 255.0 reduce-scatter.1
where the time goes:
time: 508 us; the launch traced here: 507 us
  waiting for transfers between devices  418 us (82%)
  blocking collectives  35.3 us (7%)
  starting transfers between devices  23 us (5%)
  between operations  14.2 us (3%)
  matrix products  8.49 us (2%)
  local copies, waits for them, and re-layouts  5.76 us (1%)
    reduce_scatter x1, waiting for transfers between devices, per_device(): lax.psum_scatter(lax.dot_general(columns, cotangent, (((0,), (0,)), ((),...  253 us
    all_gather x1, waiting for transfers between devices, per_device(): lax.all_gather(local_shard, 'fsdp', axis=0, tiled=True)  140 us
    all_gather x1, blocking collectives, per_device(): new_global = lax.all_gather(new_share, 'replica', axis=1, tiled=True)  35.3 us
    all_to_all x1, starting transfers between devices, per_device(): lax.all_to_all(scale_send, 'replica', split_axis=0, concat_axis=0, tiled=...  18.2 us
    all_to_all x1, waiting for transfers between devices, per_device(): lax.all_to_all(quant_send, 'replica', split_axis=0, concat_axis=0, tiled=...  13.1 us
    all_to_all x1, waiting for transfers between devices, per_device(): lax.all_to_all(scale_send, 'replica', split_axis=0, concat_axis=0, tiled=...  10.7 us
  transfers between devices with their start and end apart: 4, of which 4 were waited for; matrix products, arithmetic and copies ran while one was open for 3% of the time, Pallas kernels for 0%

commit v1 on v0

v1 whole, which is shorter than its diff:
```python
import functools

import jax
import jax.numpy as jnp
from jax import lax
from jax.experimental import pallas as pl
from jax.experimental.pallas import tpu as pltpu
from jax.sharding import PartitionSpec as P

MESH = pl.DeviceIdType.MESH
BLOCK = 64
NX = 4
NZ = 8
NB = 8
ROWS = 64
KV = 512
D = 2048
TOK = 256
HALF = ROWS // 2
COL = NZ * ROWS

outer_rate = 0.7
outer_momentum = 0.9
scale_epsilon = 1e-06

F32 = jnp.float32
BF16 = jnp.bfloat16


def kernel(
    l_hbm, g_hbm, m_hbm, a_hbm, c_hbm,
    kv_hbm, ig_hbm, wg_hbm, ng_hbm, nm_hbm,
    a, ct, w, g, mom, kv, ig, wg, ng, nm,
    s1s, s1r, s2s, s2r, keep, xs, zs, zr, oms, omr, ps, pr, ngs, ngr,
    lsem, osem,
    s1ss, s1rs, s2ss, s2rs, zss, zrs, gzs, gzr, gxs, gxr, ghs, ghr, oas, oar, pss, prs, ogs, ogr,
):
    r = lax.axis_index("replica")
    f = lax.axis_index("fsdp")
    x = f // NZ
    j = f % NZ
    zh = r // NB
    b = r % NB

    def fs(xx, jj):
        return (r, (xx + NX) % NX * NZ + jj)

    def rowof(xx, q):
        return pl.ds(pl.multiple_of(((xx + NX) % NX * NZ + q) * ROWS, ROWS), ROWS)

    def halfof(xx, q, h):
        return pl.ds(pl.multiple_of(((xx + NX) % NX * NZ + q) * ROWS + h * HALF, HALF), HALF)

    def rcopy(src, dst, ss, rs, device):
        return pltpu.make_async_remote_copy(
            src_ref=src, dst_ref=dst, send_sem=ss, recv_sem=rs, device_id=device, device_id_type=MESH
        )

    in_a = pltpu.make_async_copy(a_hbm, a, lsem.at[0])
    in_c = pltpu.make_async_copy(c_hbm, ct, lsem.at[1])
    in_w = pltpu.make_async_copy(l_hbm, w.at[rowof(x, j)], lsem.at[2])
    in_g = pltpu.make_async_copy(g_hbm, g, lsem.at[3])
    in_m = pltpu.make_async_copy(m_hbm, mom, lsem.at[4])
    for cp in (in_a, in_c, in_w, in_g, in_m):
        cp.start()

    zpos = zh * NZ + j
    barrier = pltpu.get_barrier_semaphore()
    friends = [fs(x + 1, j), fs(x - 1, j)]
    for dz in (1, 15):
        zz = (zpos + dz) % 16
        friends.append((zz // NZ * NB + b, x * NZ + zz % NZ))
    for o in range(1, NB):
        friends.append((zh * NB + (b + o) % NB, f))
    friends.append(((r + NB) % 16, f))
    for dev in friends:
        pl.semaphore_signal(barrier, inc=1, device_id=dev, device_id_type=MESH)

    def xdev(d):
        return fs(x + 1, j) if d == 0 else fs(x - 1, j)

    def c1(d, p):
        return rcopy(s1s.at[d, p], s1r.at[d, p], s1ss.at[d, p], s1rs.at[d, p], xdev(d))

    def c2(d, p):
        return rcopy(s2s.at[d, p], s2r.at[d, p], s2ss.at[d, p], s2rs.at[d, p], xdev(d))

    def cz(d, p, h):
        rows = pl.ds(h * HALF, HALF)
        return rcopy(
            zs.at[d, p, rows], zr.at[d, p, rows], zss.at[d, h, p], zrs.at[d, h, p],
            fs(x, j + 1 if d == 0 else j - 1),
        )

    def cgz(d, q):
        return rcopy(
            w.at[rowof(x, q)], w.at[rowof(x, q)], gzs.at[d, q], gzr.at[d, q],
            fs(x, j + 1 if d == 0 else j - 1),
        )

    def cgx(d, q):
        return rcopy(w.at[rowof(x, q)], w.at[rowof(x, q)], gxs.at[d, q], gxr.at[d, q], xdev(d))

    def wgx(d, q):
        src = x - 1 if d == 0 else x + 1
        return rcopy(w.at[rowof(src, q)], w.at[rowof(src, q)], gxs.at[d, q], gxr.at[d, q], xdev(d))

    def cgh(d, q):
        src = x - 1 if d == 0 else x + 1
        return rcopy(
            w.at[halfof(src, q, d)], w.at[halfof(src, q, d)], ghs.at[d, q], ghr.at[d, q], xdev(d)
        )

    def wgh(d, q):
        return rcopy(
            w.at[halfof(x + 2, q, d)], w.at[halfof(x + 2, q, d)], ghs.at[d, q], ghr.at[d, q], xdev(d)
        )

    def coa(o):
        to = (b + o) % NB
        return rcopy(oms.at[to], omr.at[o], oas.at[o], oar.at[o], (zh * NB + to, f))

    def cog(o):
        to = (b + o) % NB
        return rcopy(ngs, ngr.at[o], ogs.at[o], ogr.at[o], (zh * NB + to, f))

    def cpartner():
        return rcopy(ps, pr, pss, prs, ((r + NB) % 16, f))

    in_a.wait()
    in_c.wait()

    def partial_block(xx):
        start = pl.multiple_of((xx + NX) % NX * COL, COL)
        return lax.dot_general(
            a[:, pl.ds(start, COL)], ct[...], (((0,), (0,)), ((), ())), preferred_element_type=F32
        )

    far = partial_block(x + 2).astype(BF16).reshape(NZ, ROWS, KV)
    s1s[0, :, 0:HALF, :] = far[:, :HALF, :]
    s1s[1, :, 0:HALF, :] = far[:, HALF:, :]
    right = partial_block(x + 1).reshape(NZ, ROWS, KV)
    s1s[0, :, HALF:, :] = right[:, HALF:, :].astype(BF16)
    keep[0] = right[:, :HALF, :]
    left = partial_block(x - 1).reshape(NZ, ROWS, KV)
    s1s[1, :, HALF:, :] = left[:, :HALF, :].astype(BF16)
    keep[1] = left[:, HALF:, :]

    pl.semaphore_wait(barrier, len(friends))

    in_w.wait()

    def z_forward(k):
        @pl.when((j - k >= 0) & (j < NZ - 1))
        def _():
            cgz(0, j - k).start()

        @pl.when((j + k < NZ) & (j > 0))
        def _():
            cgz(1, j + k).start()

    def z_arrive(k):
        @pl.when(j - k >= 0)
        def _():
            cgz(0, j - k).wait_recv()

        @pl.when(j + k < NZ)
        def _():
            cgz(1, j + k).wait_recv()

    def z_gather(k):
        z_arrive(k)
        if k < NZ - 1:
            z_forward(k)

    def pair(i):
        return (NZ - 1 - i, i)

    def start1(i):
        for p in pair(i):
            for d in range(2):
                c1(d, p).start()

    def relay(i):
        for p in pair(i):
            for d in range(2):
                c1(d, p).wait_recv()
                s2s[d, p] = (keep[d, p] + s1r[d, p, 0:HALF].astype(F32)).astype(BF16)
                c2(d, p).start()

    def settle(i):
        for p in pair(i):
            c2(0, p).wait_recv()
            xs[p, 0:HALF] += s2r[0, p].astype(F32) + s1r[1, p, HALF:].astype(F32)
            c2(1, p).wait_recv()
            xs[p, HALF:] += s2r[1, p].astype(F32) + s1r[0, p, HALF:].astype(F32)

    def z_step(s):
        pa = NZ - 1 - s + j
        pb = s - (NZ - 1) + j
        for h in range(2):
            rows = pl.ds(h * HALF, HALF)

            @pl.when(j <= s)
            def _():
                @pl.when(j == 0)
                def _():
                    zs[0, pa, rows] = xs[pa, rows]

                @pl.when(j > 0)
                def _():
                    cz(0, pa, h).wait_recv()
                    zs[0, pa, rows] = xs[pa, rows] + zr[0, pa, rows]

                cz(0, pa, h).start()

            @pl.when(pb >= 0)
            def _():
                @pl.when(j == NZ - 1)
                def _():
                    zs[1, pb, rows] = xs[pb, rows]

                @pl.when(j < NZ - 1)
                def _():
                    cz(1, pb, h).wait_recv()
                    zs[1, pb, rows] = xs[pb, rows] + zr[1, pb, rows]

                cz(1, pb, h).start()

    def z_final():
        for h in range(2):
            rows = pl.ds(h * HALF, HALF)

            @pl.when(j > 0)
            def _():
                cz(0, j, h).wait_recv()
                xs[j, rows] += zr[0, j, rows]

            @pl.when(j < NZ - 1)
            def _():
                cz(1, j, h).wait_recv()
                xs[j, rows] += zr[1, j, rows]

    def chunk(n):
        m = jnp.minimum(j, NZ - 1 - j)
        near = j - (n + 1) // 2 if n % 2 else j + n // 2
        rest = jnp.where(j < NZ // 2, n, NZ - 1 - n)
        return jnp.where(n <= 2 * m, near, rest)

    def x_send(n):
        for d in range(2):
            cgx(d, chunk(n)).start()

    def x_relay(n):
        q = chunk(n)
        for d in range(2):
            wgx(d, q).wait_recv()
            cgh(d, q).start()

    z_forward(0)
    start1(0)
    start1(1)

    xs[...] = partial_block(x).reshape(NZ, ROWS, KV)

    in_g.wait()
    in_m.wait()
    drift = g[...].astype(F32) - w[rowof(x, j), :].astype(F32)
    codes, scales = [], []
    for k in range(KV // BLOCK):
        blk = drift[:, k * BLOCK : (k + 1) * BLOCK]
        scale = (jnp.max(jnp.abs(blk), axis=1, keepdims=True) + scale_epsilon).astype(BF16)
        codes.append((blk / scale.astype(F32)).astype(BF16))
        scales.append(jnp.broadcast_to(scale.astype(F32), (ROWS, BLOCK // 2)).astype(BF16))
    hb = BLOCK // 2
    for t in range(NB):
        yy, cc = t // 2, t % 2
        cut = slice(cc * hb, cc * hb + hb)
        oms[t] = jnp.concatenate(
            [codes[yy][:, cut], codes[yy + 4][:, cut], scales[yy], scales[yy + 4]], axis=1
        )
    for o in range(1, NB):
        coa(o).start()

    def outer_sum():
        for o in range(1, NB):
            coa(o).wait_recv()
        mine = oms[b].astype(F32)
        total = mine[:, :BLOCK] * mine[:, BLOCK:]
        for o in range(1, NB):
            got = omr[o].astype(F32)
            total += got[:, :BLOCK] * got[:, BLOCK:]
        ps[0:32] = jnp.concatenate([total[:32], total[32:]], axis=1)
        m = mom[...]
        ps[32:48] = jnp.concatenate([m[:16], m[16:32], m[32:48], m[48:]], axis=1)
        cpartner().start()

    def outer_update():
        cpartner().wait_recv()
        both = ps[0:32] + pr[0:32]
        mean = jnp.concatenate([both[:, :BLOCK], both[:, BLOCK:]], axis=0) / 16.0
        pm = pr[32:48]
        theirs = jnp.concatenate([pm[:, 0:32], pm[:, 32:64], pm[:, 64:96], pm[:, 96:]], axis=0)
        ours = mom[...]
        low = zh == 0
        m64 = jnp.concatenate([jnp.where(low, ours, theirs), jnp.where(low, theirs, ours)], axis=1)
        old = jnp.zeros((ROWS, BLOCK), F32)
        for t in range(NB):
            yy, cc = t // 2, t % 2
            lo = yy * BLOCK + cc * hb
            pick = jnp.concatenate([g[:, lo : lo + hb], g[:, 256 + lo : 256 + lo + hb]], axis=1)
            old = jnp.where(b == t, pick.astype(F32), old)
        new_m = outer_momentum * m64 + mean
        share = (old - outer_rate * (mean + outer_momentum * new_m)).astype(BF16)
        nm[...] = jnp.where(low, new_m[:, :hb], new_m[:, hb:])
        ngs[...] = jnp.concatenate([share, share], axis=1)
        for o in range(1, NB):
            cog(o).start()

    def outer_collect():
        for o in range(1, NB):
            cog(o).wait_recv()
        ngr[0] = ngs[...]
        for t in range(NB):
            yy, cc = t // 2, t % 2
            lo = yy * BLOCK + cc * hb
            got = ngr[(b - t + NB) % NB]
            ng[:, lo : lo + hb] = got[:, :hb]
            ng[:, 256 + lo : 256 + lo + hb] = got[:, hb:BLOCK]

    def use_column(xx, first):
        start = pl.multiple_of((xx + NX) % NX * COL, COL)
        wc = w[pl.ds(start, COL), :]
        part = jnp.dot(a[:, pl.ds(start, COL)], wc, preferred_element_type=F32)
        if first:
            kv[...] = part
        else:
            kv[...] += part
        ig[:, pl.ds(start, COL)] = lax.dot_general(
            ct[...], wc, (((1,), (1,)), ((), ())), preferred_element_type=F32
        ).astype(BF16)

    relay(0)
    start1(2)
    z_gather(1)
    relay(1)
    start1(3)
    settle(0)
    z_step(0)
    z_gather(2)
    outer_sum()
    z_gather(3)
    relay(2)
    settle(1)
    z_step(1)
    z_gather(4)
    z_gather(5)
    relay(3)
    x_send(0)
    settle(2)
    z_step(2)
    x_send(1)
    x_send(2)
    x_send(3)
    z_gather(6)
    settle(3)
    z_step(3)
    outer_update()
    x_send(4)
    x_send(5)
    z_gather(7)
    x_send(6)
    x_send(7)
    x_relay(0)
    x_relay(1)
    z_step(4)
    x_relay(2)
    x_relay(3)
    use_column(x, True)
    z_step(5)
    x_relay(4)
    x_relay(5)
    outer_collect()
    out_ng = pltpu.make_async_copy(ng, ng_hbm, osem.at[0])
    out_nm = pltpu.make_async_copy(nm, nm_hbm, osem.at[1])
    out_ng.start()
    out_nm.start()
    z_step(6)
    x_relay(6)
    x_relay(7)
    z_final()
    wg[...] = (xs[j] * (1.0 / (TOK * NX * NZ))).astype(BF16)
    out_wg = pltpu.make_async_copy(wg, wg_hbm, osem.at[2])
    out_wg.start()
    use_column(x + 1, False)
    use_column(x - 1, False)
    for n in range(NZ):
        for d in range(2):
            wgh(d, chunk(n)).wait_recv()
    use_column(x + 2, False)
    out_ig = pltpu.make_async_copy(ig, ig_hbm, osem.at[3])
    out_ig.start()
    a[:, 0:KV] = kv[...].astype(BF16)
    out_kv = pltpu.make_async_copy(a.at[:, 0:KV], kv_hbm, osem.at[4])
    out_kv.start()

    for p in range(NZ):
        for d in range(2):
            c1(d, p).wait_send()
            c2(d, p).wait_send()
            cgx(d, p).wait_send()
            cgh(d, p).wait_send()
        for h in range(2):
            @pl.when(p > j)
            def _():
                cz(0, p, h).wait_send()

            @pl.when(p < j)
            def _():
                cz(1, p, h).wait_send()

        @pl.when((p <= j) & (j < NZ - 1))
        def _():
            cgz(0, p).wait_send()

        @pl.when((p >= j) & (j > 0))
        def _():
            cgz(1, p).wait_send()

    for o in range(1, NB):
        coa(o).wait_send()
        cog(o).wait_send()
    cpartner().wait_send()
    for cp in (out_ng, out_nm, out_wg, out_ig, out_kv):
        cp.wait()


def per_device(local_weights, global_weights, momentum, activations, kv_cotangent):
    dma = pltpu.SemaphoreType.DMA
    hbm = pl.BlockSpec(memory_space=pl.ANY)
    outs = pl.pallas_call(
        kernel,
        name="joined_step",
        out_shape=(
            jax.ShapeDtypeStruct((TOK, KV), BF16),
            jax.ShapeDtypeStruct((TOK, D), BF16),
            jax.ShapeDtypeStruct((ROWS, KV), BF16),
            jax.ShapeDtypeStruct((ROWS, KV), BF16),
            jax.ShapeDtypeStruct((ROWS, 32), F32),
        ),
        in_specs=[hbm] * 5,
        out_specs=[hbm] * 5,
        scratch_shapes=[
            pltpu.VMEM((TOK, D), BF16),
            pltpu.VMEM((TOK, KV), BF16),
            pltpu.VMEM((D, KV), BF16),
            pltpu.VMEM((ROWS, KV), BF16),
            pltpu.VMEM((ROWS, 32), F32),
            pltpu.VMEM((TOK, KV), F32),
            pltpu.VMEM((TOK, D), BF16),
            pltpu.VMEM((ROWS, KV), BF16),
            pltpu.VMEM((ROWS, KV), BF16),
            pltpu.VMEM((ROWS, 32), F32),
            pltpu.VMEM((2, NZ, ROWS, KV), BF16),
            pltpu.VMEM((2, NZ, ROWS, KV), BF16),
            pltpu.VMEM((2, NZ, HALF, KV), BF16),
            pltpu.VMEM((2, NZ, HALF, KV), BF16),
            pltpu.VMEM((2, NZ, HALF, KV), F32),
            pltpu.VMEM((NZ, ROWS, KV), F32),
            pltpu.VMEM((2, NZ, ROWS, KV), F32),
            pltpu.VMEM((2, NZ, ROWS, KV), F32),
            pltpu.VMEM((NB, ROWS, 128), BF16),
            pltpu.VMEM((NB, ROWS, 128), BF16),
            pltpu.VMEM((48, 128), F32),
            pltpu.VMEM((48, 128), F32),
            pltpu.VMEM((ROWS, 128), BF16),
            pltpu.VMEM((NB, ROWS, 128), BF16),
            dma((5,)),
            dma((5,)),
            dma((2, NZ)), dma((2, NZ)),
            dma((2, NZ)), dma((2, NZ)),
            dma((2, 2, NZ)), dma((2, 2, NZ)),
            dma((2, NZ)), dma((2, NZ)),
            dma((2, NZ)), dma((2, NZ)),
            dma((2, NZ)), dma((2, NZ)),
            dma((NB,)), dma((NB,)),
            dma(()), dma(()),
            dma((NB,)), dma((NB,)),
        ],
        compiler_params=pltpu.CompilerParams(
            collective_id=0, has_side_effects=True, vmem_limit_bytes=40 * 2**20
        ),
        cost_estimate=pl.CostEstimate(
            flops=6 * TOK * D * KV, bytes_accessed=6 * 2**20, transcendentals=0
        ),
    )(local_weights[0], global_weights, momentum, activations[0], kv_cotangent[0])
    kv, ig, wg, ng, nm = outs
    return kv[None], ig[None], wg[None], ng, nm


def solution(mesh):
    placed = (
        P("replica", "fsdp", None),
        P("fsdp", None),
        P("fsdp", "replica"),
        P("replica", "fsdp", None),
        P("replica", "fsdp", None),
    )
    return jax.shard_map(
        per_device,
        mesh=mesh,
        in_specs=placed,
        out_specs=(
            P("replica", "fsdp", None),
            P("replica", "fsdp", None),
            P("replica", "fsdp", None),
            P("fsdp", None),
            P("fsdp", "replica"),
        ),
        check_vma=False,
    )
```

time: 508 us -> 71.9 us (0.14)
  waiting for transfers between devices: 418 us -> 0 us
  Pallas kernels: 0 us -> 62.7 us
  blocking collectives: 35.3 us -> 0 us
  starting transfers between devices: 23 us -> 0 us
  between operations: 14.2 us -> 0.65 us
  matrix products: 8.49 us -> 0 us
    reduce_scatter x1 -> x0, waiting for transfers between devices: 253 us -> none  [per_device(): lax.psum_scatter(lax.dot_general(columns, cotangent, (((0,), (0,)), ((),...]
    all_gather x1 -> x0, waiting for transfers between devices: 140 us -> none  [per_device(): lax.all_gather(local_shard, 'fsdp', axis=0, tiled=True)]
    pallas_call x0 -> x1, Pallas kernels: none -> 62.7 us  [per_device(): pl.pallas_call(kernel, name='joined_step', out_shape=(jax.ShapeDtypeStruc...]
    all_gather x1 -> x0, blocking collectives: 35.3 us -> none  [per_device(): new_global = lax.all_gather(new_share, 'replica', axis=1, tiled=True)]
    all_to_all x2 -> x0, waiting for transfers between devices: 23.8 us -> none  [the longest x1 13.1 us: per_device(): lax.all_to_all(quant_send, 'replica', split_axis=0, concat_axis=0, tiled=...]
    all_to_all x2 -> x0, starting transfers between devices: 22.9 us -> none  [the longest x1 18.2 us: per_device(): lax.all_to_all(scale_send, 'replica', split_axis=0, concat_axis=0, tiled=...]
    dot_general x3 -> x0, matrix products: 8.49 us -> none  [the longest x1 3.63 us: per_device(): lax.dot_general(columns, cotangent, (((0,), (0,)), ((), ())), preferred_e...]
  transfers between devices with their start and end apart: 4 -> 0, of which waited for: 4 -> 0; matrix products, arithmetic and copies ran while one was open for 3% -> 0% of each run, Pallas kernels for 0% -> 0%
where the time goes in v1:
time: 71.9 us; the launch traced here: 71.6 us
  Pallas kernels  62.7 us (87%)
  local copies, waits for them, and re-layouts  8.26 us (11%)
    pallas_call x1, Pallas kernels, per_device(): pl.pallas_call(kernel, name='joined_step', out_shape=(jax.ShapeDtypeStruc...  62.7 us
    unnamed x14, local copies, waits for them, and re-layouts  8.26 us

profile of v1, /device:TPU:8, one launch (start us, length us, event | category | flops | bytes accessed | tf_op | source)
XLA Modules:
  0.0 71.6 jit_solution(5560995437942494567)
XLA Ops:
  0.6 0.8 %copy.10.m_hbm = f32[64,32]{1,0:T(8,128)S(1)} copy(f32[64,32]{0,1:T(8,128)} %param.7) | data formatting | bytes 16384 | tf_op args[2]
  1.4 0.0 copy-start
  1.4 1.2 %copy-done = bf16[1,256,2048]{2,1,0:T(8,128)(2,1)S(1)} copy-done((bf16[1,256,2048]{2,1,0:T(8,128)(2,1)S(1)}, bf16[1,256,2048]{2,1,0:T(8,128)(2,1)}, u32[]{:S(2)}) %copy-start) | copy-done | bytes 1048600
  2.7 0.0 copy-start.1
  2.7 0.9 %copy-done.1 = bf16[1,256,512]{2,1,0:T(8,128)(2,1)S(1)} copy-done((bf16[1,256,512]{2,1,0:T(8,128)(2,1)S(1)}, bf16[1,256,512]{2,1,0:T(8,128)(2,1)}, u32[]{:S(2)}) %copy-start.1) | copy-done | bytes 262168
  3.6 0.0 copy-start.2
  3.6 0.8 %copy-done.2 = bf16[1,64,512]{2,1,0:T(8,128)(2,1)S(1)} copy-done((bf16[1,64,512]{2,1,0:T(8,128)(2,1)S(1)}, bf16[1,64,512]{2,1,0:T(8,128)(2,1)}, u32[]{:S(2)}) %copy-start.2) | copy-done | bytes 65560
  4.4 0.0 copy-start.3
  4.5 0.8 %copy-done.3 = bf16[64,512]{1,0:T(8,128)(2,1)S(1)} copy-done((bf16[64,512]{1,0:T(8,128)(2,1)S(1)}, bf16[64,512]{1,0:T(8,128)(2,1)}, u32[]{:S(2)}) %copy-start.3) | copy-done | bytes 65560
  5.3 62.7 %joined_step.1 = (bf16[256,512]{1,0:T(8,128)(2,1)S(1)}, bf16[256,2048]{1,0:T(8,128)(2,1)S(1)}, bf16[64,512]{1,0:T(8,128)(2,1)S(1)}, bf16[64,512]{1,0:T(8,128)(2,1)S(1)}, f32[64,32]{1,0:T(8,128)S(1)}) custom-call(bf16[64,512]{1,0:T(8,128)(2,1)S(1)} %bitcast.11, bf16[64,512]{1,0:T(8,128)(2,1)S(1)} %copy-done.3, f32[64,32]{1,0:T(8,128)S(1)} %copy.10.m_hbm, ...), custom_call_target="tpu_custom_call" | custom-call | flops 1610612736 | bytes 6291456 | tf_op jit(solution)/shard_map/joined_step/pallas_call | solution.py:441
  68.0 0.7 copy.11
  68.7 0.7 copy.16
  69.4 1.0 %copy.17 = bf16[1,256,2048]{2,1,0:T(8,128)(2,1)} copy(bf16[1,256,2048]{2,1,0:T(8,128)(2,1)S(1)} %bitcast.6) | data formatting | bytes 2097152
  70.3 0.6 copy.18
  71.0 0.6 copy.19
Async XLA Ops:
  1.4 1.2 %copy-start = (bf16[1,256,2048]{2,1,0:T(8,128)(2,1)S(1)}, bf16[1,256,2048]{2,1,0:T(8,128)(2,1)}, u32[]{:S(2)}) copy-start(bf16[1,256,2048]{2,1,0:T(8,128)(2,1)} %param.8) | copy-start | bytes 3145732
  2.7 0.9 %copy-start.1 = (bf16[1,256,512]{2,1,0:T(8,128)(2,1)S(1)}, bf16[1,256,512]{2,1,0:T(8,128)(2,1)}, u32[]{:S(2)}) copy-start(bf16[1,256,512]{2,1,0:T(8,128)(2,1)} %param.9) | copy-start | bytes 786436
  3.6 0.8 %copy-start.2 = (bf16[1,64,512]{2,1,0:T(8,128)(2,1)S(1)}, bf16[1,64,512]{2,1,0:T(8,128)(2,1)}, u32[]{:S(2)}) copy-start(bf16[1,64,512]{2,1,0:T(8,128)(2,1)} %param.5) | copy-start | bytes 196612
  4.4 0.8 %copy-start.3 = (bf16[64,512]{1,0:T(8,128)(2,1)S(1)}, bf16[64,512]{1,0:T(8,128)(2,1)}, u32[]{:S(2)}) copy-start(bf16[64,512]{1,0:T(8,128)(2,1)} %g_hbm.1) | copy-start | bytes 196612

commit v2 on v0

v2 whole, which is shorter than its diff:
```python
import functools

import jax
import jax.numpy as jnp
from jax import lax
from jax.experimental import pallas as pl
from jax.experimental.pallas import tpu as pltpu
from jax.sharding import PartitionSpec as P

MESH = pl.DeviceIdType.MESH
BLOCK = 64
KERNEL_VMEM = 40 * 2**20
NX = 4
NZ = 8
NB = 8
ROWS = 64
KV = 512
D = 2048
TOK = 256
HALF = ROWS // 2
NLINE = 16
COL = NZ * ROWS

outer_rate = 0.7
outer_momentum = 0.9
scale_epsilon = 1e-06

F32 = jnp.float32
BF16 = jnp.bfloat16


def kernel(
    l_hbm, g_hbm, m_hbm, a_hbm, c_hbm,
    kv_hbm, ig_hbm, wg_hbm, ng_hbm, nm_hbm,
    a, ct, w, g, mom, kv, kvb, ig, wg, ng, nm,
    s1s, s1r, s2s, s2r, keep, xs, z1s, z1r, z2s, z2r, z3s, z3r, oms, omr, ps, pr, ngs, ngr,
    lsem, osem, near, next2, next4,
    tss, trs, oss, ors, s2ss, s2rs, z1ss, z1rs, z2ss, z2rs, z3ss, z3rs,
    gzs, gzr, gxs, gxr, ghs, ghr, oas, oar, pss, prs, ogs, ogr,
):
    r = lax.axis_index("replica")
    f = lax.axis_index("fsdp")
    x = f // NZ
    j = f % NZ
    zh = r // NB
    b = r % NB
    zpos = zh * NZ + j
    bits = (j % 2, j // 2 % 2, j // 4)

    def away(t):
        p = j
        for k in range(3):
            if t >> k & 1:
                p = p + (1 << k) * (1 - 2 * bits[k])
        return p

    def fs(xx, jj):
        return (r, (xx + NX) % NX * NZ + jj)

    def line(zz):
        return (zz // NZ * NB + b, x * NZ + zz % NZ)

    def rowof(xx, q):
        return pl.ds(pl.multiple_of(((xx + NX) % NX * NZ + q) * ROWS, ROWS), ROWS)

    def halfof(xx, q, h):
        return pl.ds(pl.multiple_of(((xx + NX) % NX * NZ + q) * ROWS + h * HALF, HALF), HALF)

    def rcopy(src, dst, ss, rs, device):
        return pltpu.make_async_remote_copy(
            src_ref=src, dst_ref=dst, send_sem=ss, recv_sem=rs, device_id=device, device_id_type=MESH
        )

    def signal(sem, device):
        pl.semaphore_signal(sem, inc=1, device_id=device, device_id_type=MESH)

    barrier = pltpu.get_barrier_semaphore()
    friends = [fs(x + 1, j), fs(x - 1, j)]
    for o in range(1, NB):
        friends.append((zh * NB + (b + o) % NB, f))
    for dev in friends:
        signal(barrier, dev)

    @pl.when(zpos > 0)
    def _():
        signal(barrier, line(zpos - 1))

    @pl.when(zpos < NLINE - 1)
    def _():
        signal(barrier, line(zpos + 1))

    in_a = pltpu.make_async_copy(a_hbm, a, lsem.at[0])
    in_c = pltpu.make_async_copy(c_hbm, ct, lsem.at[1])
    in_w = pltpu.make_async_copy(l_hbm, w.at[rowof(x, j)], lsem.at[2])
    in_g = pltpu.make_async_copy(g_hbm, g, lsem.at[3])
    in_m = pltpu.make_async_copy(m_hbm, mom, lsem.at[4])
    for cp in (in_c, in_a, in_w, in_g, in_m):
        cp.start()

    def tell1():
        @pl.when(zpos > 0)
        def _():
            signal(near.at[1], line(zpos - 1))

        @pl.when(zpos < NLINE - 1)
        def _():
            signal(near.at[0], line(zpos + 1))

    def hear1():
        @pl.when(zpos > 0)
        def _():
            pl.semaphore_wait(near.at[0], 1)

        @pl.when(zpos < NLINE - 1)
        def _():
            pl.semaphore_wait(near.at[1], 1)

    def tell2():
        @pl.when(zpos > 1)
        def _():
            signal(next2.at[1], line(zpos - 2))

        @pl.when(zpos < NLINE - 2)
        def _():
            signal(next2.at[0], line(zpos + 2))

    def hear2(inner):
        low = j < NZ // 2 if inner else j >= NZ // 2
        high = j >= NZ // 2 if inner else j < NZ // 2

        @pl.when(high & (zpos > 1))
        def _():
            pl.semaphore_wait(next2.at[0], 1)

        @pl.when(low & (zpos < NLINE - 2))
        def _():
            pl.semaphore_wait(next2.at[1], 1)

    def tell4():
        @pl.when((zpos >= 4) & (zpos < NZ + 4))
        def _():
            signal(next4, line(zpos - 4))

        @pl.when((zpos >= NZ - 4) & (zpos < NLINE - 4))
        def _():
            signal(next4, line(zpos + 4))

    def hear4():
        pl.semaphore_wait(next4, 1)

    def xdev(d):
        return fs(x + 1, j) if d == 0 else fs(x - 1, j)

    top, bottom = slice(0, HALF), slice(HALF, ROWS)

    def c_transit(d, p):
        return rcopy(s1s.at[d, p, top], s1r.at[d, p, top], tss.at[d, p], trs.at[d, p], xdev(d))

    def c_own(d, p):
        return rcopy(s1s.at[d, p, bottom], s1r.at[d, p, bottom], oss.at[d, p], ors.at[d, p], xdev(d))

    def c_sum(d, p):
        return rcopy(s2s.at[d, p], s2r.at[d, p], s2ss.at[d, p], s2rs.at[d, p], xdev(d))

    def cz1(t):
        return rcopy(z1s.at[t // 2], z1r.at[t // 2], z1ss.at[t // 2], z1rs.at[t // 2], fs(x, away(1)))

    def cz2(t):
        return rcopy(z2s.at[t // 4], z2r.at[t // 4], z2ss.at[t // 4], z2rs.at[t // 4], fs(x, away(2)))

    def cz3():
        return rcopy(z3s, z3r, z3ss, z3rs, fs(x, away(4)))

    def cgz(t):
        k = t & -t
        rows = rowof(x, away(t - k))
        return rcopy(w.at[rows], w.at[rows], gzs.at[t], gzr.at[t], fs(x, away(k)))

    def wgz(t):
        rows = rowof(x, away(t))
        return rcopy(w.at[rows], w.at[rows], gzs.at[t], gzr.at[t], fs(x, away(t & -t)))

    def cgx(d, q):
        return rcopy(w.at[rowof(x, q)], w.at[rowof(x, q)], gxs.at[d, q], gxr.at[d, q], xdev(d))

    def wgx(d, q):
        src = x - 1 if d == 0 else x + 1
        return rcopy(w.at[rowof(src, q)], w.at[rowof(src, q)], gxs.at[d, q], gxr.at[d, q], xdev(d))

    def cgh(d, q):
        src = x - 1 if d == 0 else x + 1
        return rcopy(
            w.at[halfof(src, q, d)], w.at[halfof(src, q, d)], ghs.at[d, q], ghr.at[d, q], xdev(d)
        )

    def wgh(d, q):
        return rcopy(
            w.at[halfof(x + 2, q, d)], w.at[halfof(x + 2, q, d)], ghs.at[d, q], ghr.at[d, q], xdev(d)
        )

    def coa(o):
        to = (b + o) % NB
        return rcopy(oms.at[to], omr.at[o], oas.at[o], oar.at[o], (zh * NB + to, f))

    def cog(o):
        to = (b + o) % NB
        return rcopy(ngs, ngr.at[o], ogs.at[o], ogr.at[o], (zh * NB + to, f))

    def cpartner():
        return rcopy(ps, pr, pss, prs, ((r + NB) % (2 * NB), f))

    def partial_block(xx):
        start = pl.multiple_of((xx + NX) % NX * COL, COL)
        return lax.dot_general(
            a[:, pl.ds(start, COL)], ct[...], (((0,), (0,)), ((), ())), preferred_element_type=F32
        ).reshape(NZ, ROWS, KV)

    in_c.wait()
    in_a.wait()
    far = partial_block(x + 2).astype(BF16)
    s1s[0, :, 0:HALF, :] = far[:, :HALF, :]
    s1s[1, :, 0:HALF, :] = far[:, HALF:, :]
    in_w.wait()
    pl.semaphore_wait(barrier, len(friends) + jnp.minimum(zpos, 1) + jnp.minimum(NLINE - 1 - zpos, 1))
    tell1()
    order = (7, 6, 5, 4, 3, 2, 1, 0)
    for t in order:
        for d in range(2):
            c_transit(d, away(t)).start()
    cgz(1).start()

    right = partial_block(x + 1)
    s1s[0, :, HALF:, :] = right[:, HALF:, :].astype(BF16)
    keep[0] = right[:, :HALF, :]
    left = partial_block(x - 1)
    s1s[1, :, HALF:, :] = left[:, :HALF, :].astype(BF16)
    keep[1] = left[:, HALF:, :]

    def relay(t):
        p = away(t)
        for d in range(2):
            c_own(d, p).start()
            c_transit(d, p).wait_recv()
            s2s[d, p] = (keep[d, p] + s1r[d, p, top].astype(F32)).astype(BF16)
            c_sum(d, p).start()

    def settle(t):
        p = away(t)
        for d in range(2):
            c_own(d, p).wait_recv()
        for d in range(2):
            c_sum(d, p).wait_recv()
        xs[p, top] += s2r[0, p].astype(F32) + s1r[1, p, bottom].astype(F32)
        xs[p, bottom] += s2r[1, p].astype(F32) + s1r[0, p, bottom].astype(F32)
        if t % 2:
            z1s[t // 2] = xs[p].astype(BF16)
            cz1(t).start()

    def round1(t):
        cz1(t + 1).wait_recv()
        xs[away(t)] += z1r[t // 2].astype(F32)
        if t % 4 == 2:
            z2s[t // 4] = xs[away(t)].astype(BF16)
            cz2(t).start()

    def round2(t):
        cz2(t + 2).wait_recv()
        xs[away(t)] += z2r[t // 4].astype(F32)
        if t == 4:
            z3s[...] = xs[away(t)]
            cz3().start()

    def z_arrive(t, *onward):
        wgz(t).wait_recv()
        for k in onward:
            cgz(t + k).start()

    def x_send(t):
        for d in range(2):
            cgx(d, away(t)).start()

    def x_relay(t):
        q = away(t)
        for d in range(2):
            wgx(d, q).wait_recv()
            cgh(d, q).start()

    hb = BLOCK // 2

    def outer_send():
        in_g.wait()
        in_m.wait()
        drift = g[...].astype(F32) - w[rowof(x, j), :].astype(F32)
        codes, scales = [], []
        for k in range(KV // BLOCK):
            blk = drift[:, k * BLOCK : (k + 1) * BLOCK]
            scale = (jnp.max(jnp.abs(blk), axis=1, keepdims=True) + scale_epsilon).astype(BF16)
            codes.append((blk / scale.astype(F32)).astype(BF16))
            scales.append(jnp.broadcast_to(scale.astype(F32), (ROWS, hb)).astype(BF16))
        for t in range(NB):
            yy, cc = t // 2, t % 2
            cut = slice(cc * hb, cc * hb + hb)
            oms[t] = jnp.concatenate(
                [codes[yy][:, cut], codes[yy + 4][:, cut], scales[yy], scales[yy + 4]], axis=1
            )
        for o in range(1, NB):
            coa(o).start()

    def outer_sum():
        for o in range(1, NB):
            coa(o).wait_recv()
        mine = oms[b].astype(F32)
        total = mine[:, :BLOCK] * mine[:, BLOCK:]
        for o in range(1, NB):
            got = omr[o].astype(F32)
            total += got[:, :BLOCK] * got[:, BLOCK:]
        ps[0:32] = jnp.concatenate([total[:32], total[32:]], axis=1)
        m = mom[...].T
        ps[32:48] = jnp.concatenate([m[:16], m[16:32], m[32:48], m[48:]], axis=1)
        cpartner().start()

    def outer_update():
        cpartner().wait_recv()
        both = ps[0:32] + pr[0:32]
        mean = jnp.concatenate([both[:, :BLOCK], both[:, BLOCK:]], axis=0) / (2 * NB)
        pm = pr[32:48]
        theirs = jnp.concatenate([pm[:, 0:32], pm[:, 32:64], pm[:, 64:96], pm[:, 96:]], axis=0)
        ours = mom[...].T
        low = zh == 0
        m64 = jnp.concatenate([jnp.where(low, ours, theirs), jnp.where(low, theirs, ours)], axis=1)
        old = jnp.zeros((ROWS, BLOCK), F32)
        for t in range(NB):
            yy, cc = t // 2, t % 2
            lo = yy * BLOCK + cc * hb
            pick = jnp.concatenate([g[:, lo : lo + hb], g[:, 256 + lo : 256 + lo + hb]], axis=1)
            old = jnp.where(b == t, pick.astype(F32), old)
        new_m = outer_momentum * m64 + mean
        share = (old - outer_rate * (mean + outer_momentum * new_m)).astype(BF16)
        nm[...] = jnp.where(low, new_m[:, :hb], new_m[:, hb:]).T
        ngs[...] = jnp.concatenate([share, share], axis=1)
        for o in range(1, NB):
            cog(o).start()

    def outer_collect():
        for o in range(1, NB):
            cog(o).wait_recv()
        ngr[0] = ngs[...]
        for t in range(NB):
            yy, cc = t // 2, t % 2
            lo = yy * BLOCK + cc * hb
            got = ngr[(b - t + NB) % NB]
            ng[:, lo : lo + hb] = got[:, :hb]
            ng[:, 256 + lo : 256 + lo + hb] = got[:, hb:BLOCK]

    def out_column(n, xx):
        cols = pl.ds(pl.multiple_of((xx + NX) % NX * COL, COL), COL)
        return pltpu.make_async_copy(ig.at[:, cols], ig_hbm.at[:, cols], osem.at[n])

    def use_column(n, xx):
        start = pl.multiple_of((xx + NX) % NX * COL, COL)
        wc = w[pl.ds(start, COL), :]
        part = jnp.dot(a[:, pl.ds(start, COL)], wc, preferred_element_type=F32)
        if n == 0:
            kv[...] = part
        elif n < 3:
            kv[...] += part
        else:
            kvb[...] = (kv[...] + part).astype(BF16)
        ig[:, pl.ds(start, COL)] = lax.dot_general(
            ct[...], wc, (((1,), (1,)), ((), ())), preferred_element_type=F32
        ).astype(BF16)
        out_column(n, xx).start()

    outer_send()
    xs[...] = partial_block(x)
    hear1()
    cgz(2).start()
    tell2()
    relay(7)
    relay(6)
    relay(5)
    relay(4)
    hear2(True)
    cgz(4).start()
    relay(3)
    relay(2)
    z_arrive(1)
    z_arrive(2, 1)
    relay(1)
    relay(0)
    x_send(0)
    x_send(1)
    settle(7)
    settle(6)
    x_send(2)
    hear2(False)
    tell4()
    settle(5)
    settle(4)
    z_arrive(4, 2, 1)
    round1(6)
    z_arrive(3)
    x_send(3)
    settle(3)
    settle(2)
    round1(4)
    round1(2)
    hear4()
    outer_sum()
    z_arrive(6, 1)
    x_send(4)
    x_send(6)
    settle(1)
    settle(0)
    round2(4)
    z_arrive(5)
    x_send(5)
    z_arrive(7)
    x_send(7)
    x_relay(0)
    x_relay(1)
    use_column(0, x)
    x_relay(2)
    round1(0)
    round2(0)
    x_relay(3)
    x_relay(4)
    outer_update()
    out_nm = pltpu.make_async_copy(nm, nm_hbm, osem.at[4])
    out_nm.start()
    x_relay(6)
    x_relay(5)
    cz3().wait_recv()
    wg[...] = ((xs[j] + z3r[...]) * (1.0 / (TOK * NX * NZ))).astype(BF16)
    out_wg = pltpu.make_async_copy(wg, wg_hbm, osem.at[5])
    out_wg.start()
    x_relay(7)
    use_column(1, x + 1)
    use_column(2, x - 1)
    outer_collect()
    out_ng = pltpu.make_async_copy(ng, ng_hbm, osem.at[6])
    out_ng.start()
    for t in range(NZ):
        for d in range(2):
            wgh(d, away(t)).wait_recv()
    use_column(3, x + 2)
    out_kv = pltpu.make_async_copy(kvb, kv_hbm, osem.at[7])
    out_kv.start()

    for p in range(NZ):
        for d in range(2):
            c_transit(d, p).wait_send()
            c_own(d, p).wait_send()
            c_sum(d, p).wait_send()
            cgx(d, p).wait_send()
            cgh(d, p).wait_send()
    for t in range(1, NZ):
        cgz(t).wait_send()
    for t in (1, 3, 5, 7):
        cz1(t).wait_send()
    for t in (2, 6):
        cz2(t).wait_send()
    cz3().wait_send()
    for o in range(1, NB):
        coa(o).wait_send()
        cog(o).wait_send()
    cpartner().wait_send()
    for n, xx in enumerate((x, x + 1, x - 1, x + 2)):
        out_column(n, xx).wait()
    for cp in (out_ng, out_nm, out_wg, out_kv):
        cp.wait()


def finish(*refs):
    srcs, dsts, sem = refs[:5], refs[5:10], refs[10]
    copies = [pltpu.make_async_copy(s, d, sem.at[n]) for n, (s, d) in enumerate(zip(srcs, dsts))]
    for cp in copies:
        cp.start()
    for cp in copies:
        cp.wait()


def per_device(local_weights, global_weights, momentum, activations, kv_cotangent):
    dma = pltpu.SemaphoreType.DMA
    hbm = pl.BlockSpec(memory_space=pl.ANY)
    shapes = (
        jax.ShapeDtypeStruct((TOK, KV), BF16),
        jax.ShapeDtypeStruct((TOK, D), BF16),
        jax.ShapeDtypeStruct((ROWS, KV), BF16),
        jax.ShapeDtypeStruct((ROWS, KV), BF16),
        jax.ShapeDtypeStruct((32, ROWS), F32),
    )
    vmem = pltpu.VMEM
    outs = pl.pallas_call(
        kernel,
        name="joined_step",
        out_shape=shapes,
        in_specs=[hbm] * 5,
        out_specs=[hbm] * 5,
        scratch_shapes=[
            vmem((TOK, D), BF16),
            vmem((TOK, KV), BF16),
            vmem((D, KV), BF16),
            vmem((ROWS, KV), BF16),
            vmem((32, ROWS), F32),
            vmem((TOK, KV), F32),
            vmem((TOK, KV), BF16),
            vmem((TOK, D), BF16),
            vmem((ROWS, KV), BF16),
            vmem((ROWS, KV), BF16),
            vmem((32, ROWS), F32),
            vmem((2, NZ, ROWS, KV), BF16),
            vmem((2, NZ, ROWS, KV), BF16),
            vmem((2, NZ, HALF, KV), BF16),
            vmem((2, NZ, HALF, KV), BF16),
            vmem((2, NZ, HALF, KV), F32),
            vmem((NZ, ROWS, KV), F32),
            vmem((4, ROWS, KV), BF16),
            vmem((4, ROWS, KV), BF16),
            vmem((2, ROWS, KV), BF16),
            vmem((2, ROWS, KV), BF16),
            vmem((ROWS, KV), F32),
            vmem((ROWS, KV), F32),
            vmem((NB, ROWS, 128), BF16),
            vmem((NB, ROWS, 128), BF16),
            vmem((48, 128), F32),
            vmem((48, 128), F32),
            vmem((ROWS, 128), BF16),
            vmem((NB, ROWS, 128), BF16),
            dma((5,)),
            dma((8,)),
            pltpu.SemaphoreType.REGULAR((2,)),
            pltpu.SemaphoreType.REGULAR((2,)),
            pltpu.SemaphoreType.REGULAR,
            dma((2, NZ)), dma((2, NZ)),
            dma((2, NZ)), dma((2, NZ)),
            dma((2, NZ)), dma((2, NZ)),
            dma((4,)), dma((4,)),
            dma((2,)), dma((2,)),
            dma(()), dma(()),
            dma((NZ,)), dma((NZ,)),
            dma((2, NZ)), dma((2, NZ)),
            dma((2, NZ)), dma((2, NZ)),
            dma((NB,)), dma((NB,)),
            dma(()), dma(()),
            dma((NB,)), dma((NB,)),
        ],
        compiler_params=pltpu.CompilerParams(
            collective_id=0, has_side_effects=True, vmem_limit_bytes=KERNEL_VMEM
        ),
        cost_estimate=pl.CostEstimate(
            flops=6 * TOK * D * KV, bytes_accessed=6 * 2**20, transcendentals=0
        ),
    )(local_weights[0], global_weights, momentum.T, activations[0], kv_cotangent[0])
    kv, ig, wg, ng, nm = pl.pallas_call(
        finish,
        name="finish",
        out_shape=shapes,
        in_specs=[hbm] * 5,
        out_specs=[hbm] * 5,
        scratch_shapes=[dma((5,))],
        compiler_params=pltpu.CompilerParams(vmem_limit_bytes=2**20),
    )(*outs)
    return kv[None], ig[None], wg[None], ng, nm.T


def solution(mesh):
    placed = (
        P("replica", "fsdp", None),
        P("fsdp", None),
        P("fsdp", "replica"),
        P("replica", "fsdp", None),
        P("replica", "fsdp", None),
    )
    return jax.shard_map(
        per_device,
        mesh=mesh,
        in_specs=placed,
        out_specs=(
            P("replica", "fsdp", None),
            P("replica", "fsdp", None),
            P("replica", "fsdp", None),
            P("fsdp", None),
            P("fsdp", "replica"),
        ),
        check_vma=False,
    )
```

time: 508 us -> 60.9 us (0.12)
  the two profiles are of different devices: /device:TPU:8 before, /device:TPU:56 now
where the time goes in v2:
time: 60.9 us; the launch traced here: 60.5 us
  Pallas kernels  55.3 us (91%)
  local copies, waits for them, and re-layouts  4.56 us (7%)
  between operations  0.65 us (1%)
    pallas_call x1, Pallas kernels, per_device(): pl.pallas_call(kernel, name='joined_step', out_shape=shapes, in_specs=[hb...  54.2 us
    unnamed x10, local copies, waits for them, and re-layouts  4.56 us

profile of v2, /device:TPU:56, one launch (start us, length us, event | category | flops | bytes accessed | tf_op | source)
XLA Modules:
  0.0 60.5 jit_solution(15794859165960539407)
XLA Ops:
  0.6 0.0 copy-start
  0.6 1.2 %copy-done = bf16[1,256,2048]{2,1,0:T(8,128)(2,1)S(1)} copy-done((bf16[1,256,2048]{2,1,0:T(8,128)(2,1)S(1)}, bf16[1,256,2048]{2,1,0:T(8,128)(2,1)}, u32[]{:S(2)}) %copy-start) | copy-done | bytes 1048600
  1.9 0.0 copy-start.1
  1.9 0.9 %copy-done.1 = bf16[1,256,512]{2,1,0:T(8,128)(2,1)S(1)} copy-done((bf16[1,256,512]{2,1,0:T(8,128)(2,1)S(1)}, bf16[1,256,512]{2,1,0:T(8,128)(2,1)}, u32[]{:S(2)}) %copy-start.1) | copy-done | bytes 262168
  2.8 0.0 copy-start.2
  2.8 0.8 %copy-done.2 = bf16[1,64,512]{2,1,0:T(8,128)(2,1)S(1)} copy-done((bf16[1,64,512]{2,1,0:T(8,128)(2,1)S(1)}, bf16[1,64,512]{2,1,0:T(8,128)(2,1)}, u32[]{:S(2)}) %copy-start.2) | copy-done | bytes 65560
  3.6 0.0 copy-start.3
  3.7 0.8 %copy-done.3 = bf16[64,512]{1,0:T(8,128)(2,1)S(1)} copy-done((bf16[64,512]{1,0:T(8,128)(2,1)S(1)}, bf16[64,512]{1,0:T(8,128)(2,1)}, u32[]{:S(2)}) %copy-start.3) | copy-done | bytes 65560
  4.5 0.0 copy-start.4
  4.5 0.7 %copy-done.4 = f32[64,32]{0,1:T(8,128)S(1)} copy-done((f32[64,32]{0,1:T(8,128)S(1)}, f32[64,32]{0,1:T(8,128)}, u32[]{:S(2)}) %copy-start.4) | copy-done | bytes 8216
  5.2 54.2 %joined_step.1 = (bf16[256,512]{1,0:T(8,128)(2,1)S(1)}, bf16[256,2048]{1,0:T(8,128)(2,1)S(1)}, bf16[64,512]{1,0:T(8,128)(2,1)S(1)}, bf16[64,512]{1,0:T(8,128)(2,1)S(1)}, f32[32,64]{1,0:T(8,128)S(1)}) custom-call(bf16[64,512]{1,0:T(8,128)(2,1)S(1)} %bitcast.10, bf16[64,512]{1,0:T(8,128)(2,1)S(1)} %copy-done.3, f32[32,64]{1,0:T(8,128)S(1)} %bitcast.11, ...), custom_call_target="tpu_custom_call" | custom-call | flops 1610612736 | bytes 6291456 | tf_op jit(solution)/shard_map/joined_step/pallas_call | solution.py:494
  59.4 1.1 %finish.1 = (bf16[256,512]{1,0:T(8,128)(2,1)}, bf16[256,2048]{1,0:T(8,128)(2,1)}, bf16[64,512]{1,0:T(8,128)(2,1)}, bf16[64,512]{1,0:T(8,128)(2,1)}, f32[32,64]{1,0:T(8,128)}) custom-call(bf16[256,512]{1,0:T(8,128)(2,1)S(1)} %get-tuple-element.15.refs_0_, bf16[256,2048]{1,0:T(8,128)(2,1)S(1)} %get-tuple-element.16.refs_1_, ...), custom_call_target="tpu_custom_call" | custom-call | tf_op jit(solution)/shard_map/finish/pallas_call | solution.py:555
Async XLA Ops:
  0.6 1.2 %copy-start = (bf16[1,256,2048]{2,1,0:T(8,128)(2,1)S(1)}, bf16[1,256,2048]{2,1,0:T(8,128)(2,1)}, u32[]{:S(2)}) copy-start(bf16[1,256,2048]{2,1,0:T(8,128)(2,1)} %param.8) | copy-start | bytes 3145732
  1.9 0.9 %copy-start.1 = (bf16[1,256,512]{2,1,0:T(8,128)(2,1)S(1)}, bf16[1,256,512]{2,1,0:T(8,128)(2,1)}, u32[]{:S(2)}) copy-start(bf16[1,256,512]{2,1,0:T(8,128)(2,1)} %param.9) | copy-start | bytes 786436
  2.8 0.8 %copy-start.2 = (bf16[1,64,512]{2,1,0:T(8,128)(2,1)S(1)}, bf16[1,64,512]{2,1,0:T(8,128)(2,1)}, u32[]{:S(2)}) copy-start(bf16[1,64,512]{2,1,0:T(8,128)(2,1)} %param.5) | copy-start | bytes 196612
  3.6 0.8 %copy-start.3 = (bf16[64,512]{1,0:T(8,128)(2,1)S(1)}, bf16[64,512]{1,0:T(8,128)(2,1)}, u32[]{:S(2)}) copy-start(bf16[64,512]{1,0:T(8,128)(2,1)} %g_hbm.1) | copy-start | bytes 196612
  4.5 0.7 %copy-start.4 = (f32[64,32]{0,1:T(8,128)S(1)}, f32[64,32]{0,1:T(8,128)}, u32[]{:S(2)}) copy-start(f32[64,32]{0,1:T(8,128)} %param.7) | copy-start | bytes 24580

commit v3 on v2

--- a/solution.py
+++ b/solution.py
@@ -9,7 +9,7 @@
 
 MESH = pl.DeviceIdType.MESH
 BLOCK = 64
-KERNEL_VMEM = 40 * 2**20
+KERNEL_VMEM = 52 * 2**20
 NX = 4
 NZ = 8
 NB = 8
@@ -30,7 +30,7 @@
 
 
 def kernel(
-    l_hbm, g_hbm, m_hbm, a_hbm, c_hbm,
+    m_hbm, a_hbm, b_hbm,
     kv_hbm, ig_hbm, wg_hbm, ng_hbm, nm_hbm,
     a, ct, w, g, mom, kv, kvb, ig, wg, ng, nm,
     s1s, s1r, s2s, s2r, keep, xs, z1s, z1r, z2s, z2r, z3s, z3r, oms, omr, ps, pr, ngs, ngr,
@@ -90,11 +90,11 @@
         signal(barrier, line(zpos + 1))
 
     in_a = pltpu.make_async_copy(a_hbm, a, lsem.at[0])
-    in_c = pltpu.make_async_copy(c_hbm, ct, lsem.at[1])
-    in_w = pltpu.make_async_copy(l_hbm, w.at[rowof(x, j)], lsem.at[2])
-    in_g = pltpu.make_async_copy(g_hbm, g, lsem.at[3])
+    in_c = pltpu.make_async_copy(b_hbm.at[0:TOK], ct, lsem.at[1])
+    in_w = pltpu.make_async_copy(b_hbm.at[TOK : TOK + ROWS], w.at[rowof(x, j)], lsem.at[2])
+    in_g = pltpu.make_async_copy(b_hbm.at[TOK + ROWS : TOK + 2 * ROWS], g, lsem.at[3])
     in_m = pltpu.make_async_copy(m_hbm, mom, lsem.at[4])
-    for cp in (in_c, in_a, in_w, in_g, in_m):
+    for cp in (in_a, in_c, in_w, in_g, in_m):
         cp.start()
 
     def tell1():
@@ -171,14 +171,11 @@
     def cz3():
         return rcopy(z3s, z3r, z3ss, z3rs, fs(x, away(4)))
 
-    def cgz(t):
-        k = t & -t
-        rows = rowof(x, away(t - k))
-        return rcopy(w.at[rows], w.at[rows], gzs.at[t], gzr.at[t], fs(x, away(k)))
-
-    def wgz(t):
-        rows = rowof(x, away(t))
-        return rcopy(w.at[rows], w.at[rows], gzs.at[t], gzr.at[t], fs(x, away(t & -t)))
+    def cgz(d, q, h):
+        rows = halfof(x, q, h)
+        return rcopy(
+            w.at[rows], w.at[rows], gzs.at[d, h, q], gzr.at[d, h, q], fs(x, j + 1 if d == 0 else j - 1)
+        )
 
     def cgx(d, q):
         return rcopy(w.at[rowof(x, q)], w.at[rowof(x, q)], gxs.at[d, q], gxr.at[d, q], xdev(d))
@@ -208,6 +205,15 @@
 
     def cpartner():
         return rcopy(ps, pr, pss, prs, ((r + NB) % (2 * NB), f))
+
+    def z_forward(k, h):
+        @pl.when((j - k >= 0) & (j < NZ - 1))
+        def _():
+            cgz(0, j - k, h).start()
+
+        @pl.when((j + k < NZ) & (j > 0))
+        def _():
+            cgz(1, j + k, h).start()
 
     def partial_block(xx):
         start = pl.multiple_of((xx + NX) % NX * COL, COL)
@@ -227,7 +233,8 @@
     for t in order:
         for d in range(2):
             c_transit(d, away(t)).start()
-    cgz(1).start()
+    z_forward(0, 0)
+    z_forward(0, 1)
 
     right = partial_block(x + 1)
     s1s[0, :, HALF:, :] = right[:, HALF:, :].astype(BF16)
@@ -267,20 +274,35 @@
         cz2(t + 2).wait_recv()
         xs[away(t)] += z2r[t // 4].astype(F32)
         if t == 4:
-            z3s[...] = xs[away(t)]
+            z3s[...] = xs[away(t)].astype(BF16)
             cz3().start()
 
-    def z_arrive(t, *onward):
-        wgz(t).wait_recv()
-        for k in onward:
-            cgz(t + k).start()
-
-    def x_send(t):
-        for d in range(2):
-            cgx(d, away(t)).start()
-
-    def x_relay(t):
-        q = away(t)
+    def z_gather(k):
+        for h in range(2):
+
+            @pl.when(j - k >= 0)
+            def _():
+                cgz(0, j - k, h).wait_recv()
+
+            @pl.when(j + k < NZ)
+            def _():
+                cgz(1, j + k, h).wait_recv()
+
+            if k < NZ - 1:
+                z_forward(k, h)
+
+    def chunk(n):
+        m = jnp.minimum(j, NZ - 1 - j)
+        near = j - (n + 1) // 2 if n % 2 else j + n // 2
+        rest = jnp.where(j < NZ // 2, n, NZ - 1 - n)
+        return jnp.where(n <= 2 * m, near, rest)
+
+    def x_send(n):
+        for d in range(2):
+            cgx(d, chunk(n)).start()
+
+    def x_relay(n):
+        q = chunk(n)
         for d in range(2):
             wgx(d, q).wait_recv()
             cgh(d, q).start()
@@ -317,7 +339,12 @@
         ps[0:32] = jnp.concatenate([total[:32], total[32:]], axis=1)
         m = mom[...].T
         ps[32:48] = jnp.concatenate([m[:16], m[16:32], m[32:48], m[48:]], axis=1)
-        cpartner().start()
+
+    def outer_swap(half):
+        @pl.when(zh == half)
+        def _():
+            hear4()
+            cpartner().start()
 
     def outer_update():
         cpartner().wait_recv()
@@ -373,79 +400,78 @@
 
     outer_send()
     xs[...] = partial_block(x)
-    hear1()
-    cgz(2).start()
-    tell2()
     relay(7)
     relay(6)
     relay(5)
+    z_gather(1)
+    hear1()
+    tell2()
     relay(4)
-    hear2(True)
-    cgz(4).start()
     relay(3)
     relay(2)
-    z_arrive(1)
-    z_arrive(2, 1)
+    z_gather(2)
     relay(1)
     relay(0)
+    outer_sum()
+    hear2(True)
+    hear2(False)
+    tell4()
+    outer_swap(1)
+    z_gather(3)
     x_send(0)
     x_send(1)
+    x_send(2)
+    x_send(3)
     settle(7)
     settle(6)
-    x_send(2)
-    hear2(False)
-    tell4()
+    z_gather(4)
+    x_send(4)
     settle(5)
+    round1(6)
     settle(4)
-    z_arrive(4, 2, 1)
-    round1(6)
-    z_arrive(3)
-    x_send(3)
+    z_gather(5)
+    x_send(5)
     settle(3)
+    round1(4)
     settle(2)
-    round1(4)
-    round1(2)
-    hear4()
-    outer_sum()
-    z_arrive(6, 1)
-    x_send(4)
+    z_gather(6)
     x_send(6)
+    round2(4)
     settle(1)
     settle(0)
-    round2(4)
-    z_arrive(5)
-    x_send(5)
-    z_arrive(7)
+    z_gather(7)
     x_send(7)
+    round1(2)
     x_relay(0)
+    outer_swap(0)
     x_relay(1)
-    use_column(0, x)
+    round1(0)
     x_relay(2)
-    round1(0)
     round2(0)
     x_relay(3)
+    use_column(0, x)
     x_relay(4)
+    x_relay(5)
+    x_relay(6)
+    x_relay(7)
+    use_column(1, x + 1)
+    use_column(2, x - 1)
     outer_update()
     out_nm = pltpu.make_async_copy(nm, nm_hbm, osem.at[4])
     out_nm.start()
-    x_relay(6)
-    x_relay(5)
     cz3().wait_recv()
-    wg[...] = ((xs[j] + z3r[...]) * (1.0 / (TOK * NX * NZ))).astype(BF16)
+    wg[...] = ((xs[j] + z3r[...].astype(F32)) * (1.0 / (TOK * NX * NZ))).astype(BF16)
     out_wg = pltpu.make_async_copy(wg, wg_hbm, osem.at[5])
     out_wg.start()
-    x_relay(7)
-    use_column(1, x + 1)
-    use_column(2, x - 1)
-    outer_collect()
-    out_ng = pltpu.make_async_copy(ng, ng_hbm, osem.at[6])
-    out_ng.start()
     for t in range(NZ):
         for d in range(2):
             wgh(d, away(t)).wait_recv()
     use_column(3, x + 2)
     out_kv = pltpu.make_async_copy(kvb, kv_hbm, osem.at[7])
     out_kv.start()
+    outer_collect()
+    out_ng = pltpu.make_async_copy(ng, ng_hbm, osem.at[6])
+    out_ng.start()
 
     for p in range(NZ):
         for d in range(2):
@@ -454,8 +480,17 @@
             c_sum(d, p).wait_send()
             cgx(d, p).wait_send()
             cgh(d, p).wait_send()
-    for t in range(1, NZ):
-        cgz(t).wait_send()
+    for q in range(NZ):
+        @pl.when((q <= j) & (j < NZ - 1))
+        def _():
+            cgz(0, q, 0).wait_send()
+            cgz(0, q, 1).wait_send()
+
+        @pl.when((q >= j) & (j > 0))
+        def _():
+            cgz(1, q, 0).wait_send()
+            cgz(1, q, 1).wait_send()
+
     for t in (1, 3, 5, 7):
         cz1(t).wait_send()
     for t in (2, 6):
@@ -491,11 +526,12 @@
         jax.ShapeDtypeStruct((32, ROWS), F32),
     )
     vmem = pltpu.VMEM
+    bundle = jnp.concatenate([kv_cotangent[0], local_weights[0], global_weights], axis=0)
     outs = pl.pallas_call(
         kernel,
         name="joined_step",
         out_shape=shapes,
-        in_specs=[hbm] * 5,
+        in_specs=[hbm] * 3,
         out_specs=[hbm] * 5,
         scratch_shapes=[
             vmem((TOK, D), BF16),
@@ -519,8 +555,8 @@
             vmem((4, ROWS, KV), BF16),
             vmem((2, ROWS, KV), BF16),
             vmem((2, ROWS, KV), BF16),
-            vmem((ROWS, KV), F32),
-            vmem((ROWS, KV), F32),
+            vmem((ROWS, KV), BF16),
+            vmem((ROWS, KV), BF16),
             vmem((NB, ROWS, 128), BF16),
             vmem((NB, ROWS, 128), BF16),
             vmem((48, 128), F32),
@@ -538,7 +574,7 @@
             dma((4,)), dma((4,)),
             dma((2,)), dma((2,)),
             dma(()), dma(()),
-            dma((NZ,)), dma((NZ,)),
+            dma((2, 2, NZ)), dma((2, 2, NZ)),
             dma((2, NZ)), dma((2, NZ)),
             dma((2, NZ)), dma((2, NZ)),
             dma((NB,)), dma((NB,)),
@@ -551,7 +587,7 @@
         cost_estimate=pl.CostEstimate(
             flops=6 * TOK * D * KV, bytes_accessed=6 * 2**20, transcendentals=0
         ),
-    )(local_weights[0], global_weights, momentum.T, activations[0], kv_cotangent[0])
+    )(momentum.T, activations[0], bundle)
     kv, ig, wg, ng, nm = pl.pallas_call(
         finish,
         name="finish",

time: 60.9 us -> 54.7 us (0.90)
  the two profiles are of different devices: /device:TPU:56 before, /device:TPU:1 now
where the time goes in v3:
time: 54.7 us; the launch traced here: 54.5 us
  Pallas kernels  52.8 us (97%)
  other arithmetic  1.06 us (2%)
  between operations  0.66 us (1%)
    pallas_call x1, Pallas kernels, per_device(): pl.pallas_call(kernel, name='joined_step', out_shape=shapes, in_specs=[hb...  51.6 us
    pallas_call x1, Pallas kernels, per_device(): pl.pallas_call(finish, name='finish', out_shape=shapes, in_specs=[hbm] *...  1.13 us

profile of v3, /device:TPU:1, one launch (start us, length us, event | category | flops | bytes accessed | tf_op | source)
XLA Modules:
  0.0 54.5 jit_solution(840570306132458177)
XLA Ops:
  0.6 0.0 copy-start
  0.6 1.1 %pad_maximum_fusion.b_hbm = bf16[384,512]{1,0:T(8,128)(2,1)S(1)} fusion(bf16[64,512]{1,0:T(8,128)(2,1)} %param.6, bf16[64,512]{1,0:T(8,128)(2,1)} %bitcast.10, bf16[256,512]{1,0:T(8,128)(2,1)} %bitcast.9), kind=kLoop, calls=%fused_computation | loop fusion | flops 1179648 | bytes 786432 | tf_op jit(solution)/shard_map/concatenate | solution.py:529
  1.7 0.0 copy-done
  1.7 51.6 %joined_step.1 = (bf16[256,512]{1,0:T(8,128)(2,1)S(1)}, bf16[256,2048]{1,0:T(8,128)(2,1)S(1)}, bf16[64,512]{1,0:T(8,128)(2,1)S(1)}, bf16[64,512]{1,0:T(8,128)(2,1)S(1)}, f32[32,64]{1,0:T(8,128)S(1)}) custom-call(f32[32,64]{1,0:T(8,128)S(1)} %bitcast.8, bf16[256,2048]{1,0:T(8,128)(2,1)} %bitcast.11, bf16[384,512]{1,0:T(8,128)(2,1)S(1)} %pad_maximum_fusion.b_hbm), custom_call_target="tpu_custom_call" | custom-call | flops 1610612736 | bytes 6291456 | tf_op jit(solution)/shard_map/joined_step/pallas_call | solution.py:530
  53.4 1.1 %finish.1 = (bf16[256,512]{1,0:T(8,128)(2,1)}, bf16[256,2048]{1,0:T(8,128)(2,1)}, bf16[64,512]{1,0:T(8,128)(2,1)}, bf16[64,512]{1,0:T(8,128)(2,1)}, f32[32,64]{1,0:T(8,128)}) custom-call(bf16[256,512]{1,0:T(8,128)(2,1)S(1)} %get-tuple-element.15.refs_0_, bf16[256,2048]{1,0:T(8,128)(2,1)S(1)} %get-tuple-element.16.refs_1_, ...), custom_call_target="tpu_custom_call" | custom-call | tf_op jit(solution)/shard_map/finish/pallas_call | solution.py:591
Async XLA Ops:
  0.6 1.1 %copy-start = (f32[64,32]{0,1:T(8,128)S(1)}, f32[64,32]{0,1:T(8,128)}, u32[]{:S(2)}) copy-start(f32[64,32]{0,1:T(8,128)} %param.7) | copy-start | bytes 24580

commit v4 on v3

--- a/solution.py
+++ b/solution.py
@@ -89,12 +89,16 @@
     def _():
         signal(barrier, line(zpos + 1))
 
-    in_a = pltpu.make_async_copy(a_hbm, a, lsem.at[0])
+    def in_cols(n, xx):
+        cols = pl.ds(pl.multiple_of((xx + NX) % NX * COL, COL), COL)
+        return pltpu.make_async_copy(a_hbm.at[:, cols], a.at[:, cols], lsem.at[n])
+
+    in_a = [in_cols(n, xx) for n, xx in zip((0, 5, 6, 7), (x + 2, x + 1, x - 1, x))]
     in_c = pltpu.make_async_copy(b_hbm.at[0:TOK], ct, lsem.at[1])
     in_w = pltpu.make_async_copy(b_hbm.at[TOK : TOK + ROWS], w.at[rowof(x, j)], lsem.at[2])
     in_g = pltpu.make_async_copy(b_hbm.at[TOK + ROWS : TOK + 2 * ROWS], g, lsem.at[3])
     in_m = pltpu.make_async_copy(m_hbm, mom, lsem.at[4])
-    for cp in (in_a, in_c, in_w, in_g, in_m):
+    for cp in (in_w, in_c, *in_a, in_g, in_m):
         cp.start()
 
     def tell1():
@@ -222,23 +226,28 @@
         ).reshape(NZ, ROWS, KV)
 
     in_c.wait()
-    in_a.wait()
+    in_a[0].wait()
     far = partial_block(x + 2).astype(BF16)
     s1s[0, :, 0:HALF, :] = far[:, :HALF, :]
     s1s[1, :, 0:HALF, :] = far[:, HALF:, :]
     in_w.wait()
     pl.semaphore_wait(barrier, len(friends) + jnp.minimum(zpos, 1) + jnp.minimum(NLINE - 1 - zpos, 1))
     tell1()
-    order = (7, 6, 5, 4, 3, 2, 1, 0)
-    for t in order:
-        for d in range(2):
-            c_transit(d, away(t)).start()
+
+    def transits(*pieces):
+        for t in pieces:
+            for d in range(2):
+                c_transit(d, away(t)).start()
+
+    transits(7, 6, 5, 4)
     z_forward(0, 0)
     z_forward(0, 1)
 
+    in_a[1].wait()
     right = partial_block(x + 1)
     s1s[0, :, HALF:, :] = right[:, HALF:, :].astype(BF16)
     keep[0] = right[:, :HALF, :]
+    in_a[2].wait()
     left = partial_block(x - 1)
     s1s[1, :, HALF:, :] = left[:, :HALF, :].astype(BF16)
     keep[1] = left[:, HALF:, :]
@@ -383,6 +392,8 @@
         cols = pl.ds(pl.multiple_of((xx + NX) % NX * COL, COL), COL)
         return pltpu.make_async_copy(ig.at[:, cols], ig_hbm.at[:, cols], osem.at[n])
 
+    out_kv = pltpu.make_async_copy(kvb, kv_hbm, osem.at[7])
+
     def use_column(n, xx):
         start = pl.multiple_of((xx + NX) % NX * COL, COL)
         wc = w[pl.ds(start, COL), :]
@@ -393,93 +404,88 @@
             kv[...] += part
         else:
             kvb[...] = (kv[...] + part).astype(BF16)
+            out_kv.start()
         ig[:, pl.ds(start, COL)] = lax.dot_general(
             ct[...], wc, (((1,), (1,)), ((), ())), preferred_element_type=F32
         ).astype(BF16)
         out_column(n, xx).start()
 
     outer_send()
+    in_a[3].wait()
     xs[...] = partial_block(x)
     relay(7)
     relay(6)
+    z_gather(1)
     relay(5)
-    z_gather(1)
+    relay(4)
+    transits(3, 2, 1, 0)
     hear1()
     tell2()
-    relay(4)
-    relay(3)
-    relay(2)
     z_gather(2)
-    relay(1)
-    relay(0)
     outer_sum()
+    settle(7)
     hear2(True)
     hear2(False)
     tell4()
     outer_swap(1)
+    settle(6)
     z_gather(3)
     x_send(0)
+    settle(5)
+    relay(3)
+    relay(2)
+    relay(1)
+    relay(0)
+    round1(6)
+    settle(4)
+    z_gather(4)
     x_send(1)
     x_send(2)
     x_send(3)
-    settle(7)
-    settle(6)
-    z_gather(4)
+    settle(3)
     x_send(4)
-    settle(5)
-    round1(6)
-    settle(4)
+    round1(4)
     z_gather(5)
     x_send(5)
-    settle(3)
-    round1(4)
-    settle(2)
+    round2(4)
     z_gather(6)
     x_send(6)
-    round2(4)
+    settle(2)
     settle(1)
+    round1(2)
+    z_gather(7)
+    outer_swap(0)
+    x_send(7)
     settle(0)
-    z_gather(7)
-    x_send(7)
-    round1(2)
     x_relay(0)
-    outer_swap(0)
+    round1(0)
     x_relay(1)
-    round1(0)
+    round2(0)
     x_relay(2)
-    round2(0)
-    x_relay(3)
     use_column(0, x)
-    x_relay(4)
-    x_relay(5)
-    x_relay(6)
-    x_relay(7)
-    use_column(1, x + 1)
-    use_column(2, x - 1)
     outer_update()
     out_nm = pltpu.make_async_copy(nm, nm_hbm, osem.at[4])
     out_nm.start()
+    x_relay(3)
+    x_relay(4)
+    x_relay(5)
+    x_relay(7)
+    x_relay(6)
+    use_column(1, x + 1)
+    use_column(2, x - 1)
     cz3().wait_recv()
     wg[...] = ((xs[j] + z3r[...].astype(F32)) * (1.0 / (TOK * NX * NZ))).astype(BF16)
     out_wg = pltpu.make_async_copy(wg, wg_hbm, osem.at[5])
     out_wg.start()
-    for t in range(NZ):
-        for d in range(2):
-            wgh(d, away(t)).wait_recv()
-    use_column(3, x + 2)
-    out_kv = pltpu.make_async_copy(kvb, kv_hbm, osem.at[7])
-    out_kv.start()
     outer_collect()
     out_ng = pltpu.make_async_copy(ng, ng_hbm, osem.at[6])
     out_ng.start()
-
     for p in range(NZ):
         for d in range(2):
             c_transit(d, p).wait_send()
             c_own(d, p).wait_send()
             c_sum(d, p).wait_send()
             cgx(d, p).wait_send()
-            cgh(d, p).wait_send()
     for q in range(NZ):
         @pl.when((q <= j) & (j < NZ - 1))
         def _():
@@ -500,6 +506,14 @@
         coa(o).wait_send()
         cog(o).wait_send()
     cpartner().wait_send()
+    for t in range(NZ):
+        for d in range(2):
+            wgh(d, away(t)).wait_recv()
+    use_column(3, x + 2)
+
+    for p in range(NZ):
+        for d in range(2):
+            cgh(d, p).wait_send()
     for n, xx in enumerate((x, x + 1, x - 1, x + 2)):
         out_column(n, xx).wait()
     for cp in (out_ng, out_nm, out_wg, out_kv):
@@ -563,7 +577,7 @@
             vmem((48, 128), F32),
             vmem((ROWS, 128), BF16),
             vmem((NB, ROWS, 128), BF16),
-            dma((5,)),
+            dma((8,)),
             dma((8,)),
             pltpu.SemaphoreType.REGULAR((2,)),
             pltpu.SemaphoreType.REGULAR((2,)),

time: 54.7 us -> 50.7 us (0.927)
  Pallas kernels: 52.8 us -> 48.8 us
    pallas_call x1, Pallas kernels: 51.6 us -> 47.7 us  [per_device(): pl.pallas_call(kernel, name='joined_step', out_shape=shapes, in_specs=[hb...]
where the time goes in v4:
time: 50.7 us; the launch traced here: 50.6 us
  Pallas kernels  48.8 us (96%)
  other arithmetic  1.06 us (2%)
  between operations  0.66 us (1%)
    pallas_call x1, Pallas kernels, per_device(): pl.pallas_call(kernel, name='joined_step', out_shape=shapes, in_specs=[hb...  47.7 us
    pallas_call x1, Pallas kernels, per_device(): pl.pallas_call(finish, name='finish', out_shape=shapes, in_specs=[hbm] *...  1.13 us
    concatenate x1, other arithmetic, per_device(): jnp.concatenate([kv_cotangent[0], local_weights[0], global_weights], axis=0)  1.06 us

profile of v4, /device:TPU:1, one launch (start us, length us, event | category | flops | bytes accessed | tf_op | source)
XLA Modules:
  0.0 50.6 jit_solution(1255271540494850772)
XLA Ops:
  0.6 0.0 copy-start
  0.6 1.1 %pad_maximum_fusion.b_hbm = bf16[384,512]{1,0:T(8,128)(2,1)S(1)} fusion(bf16[64,512]{1,0:T(8,128)(2,1)} %param.6, bf16[64,512]{1,0:T(8,128)(2,1)} %bitcast.10, bf16[256,512]{1,0:T(8,128)(2,1)} %bitcast.9), kind=kLoop, calls=%fused_computation | loop fusion | flops 1179648 | bytes 786432 | tf_op jit(solution)/shard_map/concatenate | solution.py:543
  1.7 0.0 copy-done
  1.7 47.7 %joined_step.1 = (bf16[256,512]{1,0:T(8,128)(2,1)S(1)}, bf16[256,2048]{1,0:T(8,128)(2,1)S(1)}, bf16[64,512]{1,0:T(8,128)(2,1)S(1)}, bf16[64,512]{1,0:T(8,128)(2,1)S(1)}, f32[32,64]{1,0:T(8,128)S(1)}) custom-call(f32[32,64]{1,0:T(8,128)S(1)} %bitcast.8, bf16[256,2048]{1,0:T(8,128)(2,1)} %bitcast.11, bf16[384,512]{1,0:T(8,128)(2,1)S(1)} %pad_maximum_fusion.b_hbm), custom_call_target="tpu_custom_call" | custom-call | flops 1610612736 | bytes 6291456 | tf_op jit(solution)/shard_map/joined_step/pallas_call | solution.py:544
  49.4 1.1 %finish.1 = (bf16[256,512]{1,0:T(8,128)(2,1)}, bf16[256,2048]{1,0:T(8,128)(2,1)}, bf16[64,512]{1,0:T(8,128)(2,1)}, bf16[64,512]{1,0:T(8,128)(2,1)}, f32[32,64]{1,0:T(8,128)}) custom-call(bf16[256,512]{1,0:T(8,128)(2,1)S(1)} %get-tuple-element.15.refs_0_, bf16[256,2048]{1,0:T(8,128)(2,1)S(1)} %get-tuple-element.16.refs_1_, ...), custom_call_target="tpu_custom_call" | custom-call | tf_op jit(solution)/shard_map/finish/pallas_call | solution.py:605
Async XLA Ops:
  0.6 1.1 %copy-start = (f32[64,32]{0,1:T(8,128)S(1)}, f32[64,32]{0,1:T(8,128)}, u32[]{:S(2)}) copy-start(f32[64,32]{0,1:T(8,128)} %param.7) | copy-start | bytes 24580

commit v5 on v4

--- a/solution.py
+++ b/solution.py
@@ -421,8 +421,8 @@
     transits(3, 2, 1, 0)
     hear1()
     tell2()
+    outer_sum()
     z_gather(2)
-    outer_sum()
     settle(7)
     hear2(True)
     hear2(False)
@@ -451,8 +451,8 @@
     z_gather(6)
     x_send(6)
     settle(2)
+    round1(2)
     settle(1)
-    round1(2)
     z_gather(7)
     outer_swap(0)
     x_send(7)
@@ -462,24 +462,17 @@
     x_relay(1)
     round2(0)
     x_relay(2)
-    use_column(0, x)
     outer_update()
     out_nm = pltpu.make_async_copy(nm, nm_hbm, osem.at[4])
     out_nm.start()
     x_relay(3)
     x_relay(4)
     x_relay(5)
+    x_relay(6)
+    use_column(0, x)
     x_relay(7)
-    x_relay(6)
     use_column(1, x + 1)
     use_column(2, x - 1)
-    cz3().wait_recv()
-    wg[...] = ((xs[j] + z3r[...].astype(F32)) * (1.0 / (TOK * NX * NZ))).astype(BF16)
-    out_wg = pltpu.make_async_copy(wg, wg_hbm, osem.at[5])
-    out_wg.start()
-    outer_collect()
-    out_ng = pltpu.make_async_copy(ng, ng_hbm, osem.at[6])
-    out_ng.start()
     for p in range(NZ):
         for d in range(2):
             c_transit(d, p).wait_send()
@@ -510,6 +503,13 @@
         for d in range(2):
             wgh(d, away(t)).wait_recv()
     use_column(3, x + 2)
+    outer_collect()
+    out_ng = pltpu.make_async_copy(ng, ng_hbm, osem.at[6])
+    out_ng.start()
+    cz3().wait_recv()
+    wg[...] = ((xs[j] + z3r[...].astype(F32)) * (1.0 / (TOK * NX * NZ))).astype(BF16)
+    out_wg = pltpu.make_async_copy(wg, wg_hbm, osem.at[5])
+    out_wg.start()
 
     for p in range(NZ):
         for d in range(2):

time: 50.7 us -> 50.4 us (level)
  the two profiles are of different devices: /device:TPU:1 before, /device:TPU:482 now
where the time goes in v5:
time: 50.4 us; the launch traced here: 50.3 us
  Pallas kernels  48.5 us (96%)
  other arithmetic  1.06 us (2%)
  between operations  0.66 us (1%)
    pallas_call x1, Pallas kernels, per_device(): pl.pallas_call(kernel, name='joined_step', out_shape=shapes, in_specs=[hb...  47.4 us
    pallas_call x1, Pallas kernels, per_device(): pl.pallas_call(finish, name='finish', out_shape=shapes, in_specs=[hbm] *...  1.13 us
    concatenate x1, other arithmetic, per_device(): jnp.concatenate([kv_cotangent[0], local_weights[0], global_weights], axis=0)  1.06 us

profile of v5, /device:TPU:482, one launch (start us, length us, event | category | flops | bytes accessed | tf_op | source)
XLA Modules:
  0.0 50.3 jit_solution(7392467449533361329)
XLA Ops:
  0.6 0.0 copy-start
  0.6 1.1 %pad_maximum_fusion.b_hbm = bf16[384,512]{1,0:T(8,128)(2,1)S(1)} fusion(bf16[64,512]{1,0:T(8,128)(2,1)} %param.6, bf16[64,512]{1,0:T(8,128)(2,1)} %bitcast.10, bf16[256,512]{1,0:T(8,128)(2,1)} %bitcast.9), kind=kLoop, calls=%fused_computation | loop fusion | flops 1179648 | bytes 786432 | tf_op jit(solution)/shard_map/concatenate | solution.py:543
  1.7 0.0 copy-done
  1.7 47.4 %joined_step.1 = (bf16[256,512]{1,0:T(8,128)(2,1)S(1)}, bf16[256,2048]{1,0:T(8,128)(2,1)S(1)}, bf16[64,512]{1,0:T(8,128)(2,1)S(1)}, bf16[64,512]{1,0:T(8,128)(2,1)S(1)}, f32[32,64]{1,0:T(8,128)S(1)}) custom-call(f32[32,64]{1,0:T(8,128)S(1)} %bitcast.8, bf16[256,2048]{1,0:T(8,128)(2,1)} %bitcast.11, bf16[384,512]{1,0:T(8,128)(2,1)S(1)} %pad_maximum_fusion.b_hbm), custom_call_target="tpu_custom_call" | custom-call | flops 1610612736 | bytes 6291456 | tf_op jit(solution)/shard_map/joined_step/pallas_call | solution.py:544
  49.1 1.1 %finish.1 = (bf16[256,512]{1,0:T(8,128)(2,1)}, bf16[256,2048]{1,0:T(8,128)(2,1)}, bf16[64,512]{1,0:T(8,128)(2,1)}, bf16[64,512]{1,0:T(8,128)(2,1)}, f32[32,64]{1,0:T(8,128)}) custom-call(bf16[256,512]{1,0:T(8,128)(2,1)S(1)} %get-tuple-element.15.refs_0_, bf16[256,2048]{1,0:T(8,128)(2,1)S(1)} %get-tuple-element.16.refs_1_, ...), custom_call_target="tpu_custom_call" | custom-call | tf_op jit(solution)/shard_map/finish/pallas_call | solution.py:605
Async XLA Ops:
  0.6 1.1 %copy-start = (f32[64,32]{0,1:T(8,128)S(1)}, f32[64,32]{0,1:T(8,128)}, u32[]{:S(2)}) copy-start(f32[64,32]{0,1:T(8,128)} %param.7) | copy-start | bytes 24580

commit v6 on v5

--- a/solution.py
+++ b/solution.py
@@ -13,6 +13,7 @@
 NX = 4
 NZ = 8
 NB = 8
+HUB = 3
 ROWS = 64
 KV = 512
 D = 2048
@@ -34,7 +35,7 @@
     kv_hbm, ig_hbm, wg_hbm, ng_hbm, nm_hbm,
     a, ct, w, g, mom, kv, kvb, ig, wg, ng, nm,
     s1s, s1r, s2s, s2r, keep, xs, z1s, z1r, z2s, z2r, z3s, z3r, oms, omr, ps, pr, ngs, ngr,
-    lsem, osem, near, next2, next4,
+    lsem, osem, ready, near, next2, next4,
     tss, trs, oss, ors, s2ss, s2rs, z1ss, z1rs, z2ss, z2rs, z3ss, z3rs,
     gzs, gzr, gxs, gxr, ghs, ghr, oas, oar, pss, prs, ogs, ogr,
 ):
@@ -76,10 +77,17 @@
 
     barrier = pltpu.get_barrier_semaphore()
     friends = [fs(x + 1, j), fs(x - 1, j)]
-    for o in range(1, NB):
-        friends.append((zh * NB + (b + o) % NB, f))
     for dev in friends:
         signal(barrier, dev)
+
+    @pl.when(b == HUB)
+    def _():
+        for o in range(1, NB):
+            signal(barrier, (zh * NB + (HUB + o) % NB, f))
+
+    @pl.when(b != HUB)
+    def _():
+        signal(barrier, (zh * NB + HUB, f))
 
     @pl.when(zpos > 0)
     def _():
@@ -178,7 +186,7 @@
     def cgz(d, q, h):
         rows = halfof(x, q, h)
         return rcopy(
-            w.at[rows], w.at[rows], gzs.at[d, h, q], gzr.at[d, h, q], fs(x, j + 1 if d == 0 else j - 1)
+            w.at[rows], w.at[rows], gzs.at[d, h, q], gzr.at[d, h, q], fs(x, (j + (1 if d == 0 else NZ - 1)) % NZ)
         )
 
     def cgx(d, q):
@@ -231,7 +239,14 @@
     s1s[0, :, 0:HALF, :] = far[:, :HALF, :]
     s1s[1, :, 0:HALF, :] = far[:, HALF:, :]
     in_w.wait()
-    pl.semaphore_wait(barrier, len(friends) + jnp.minimum(zpos, 1) + jnp.minimum(NLINE - 1 - zpos, 1))
+    sides = jnp.minimum(zpos, 1) + jnp.minimum(NLINE - 1 - zpos, 1)
+    pl.semaphore_wait(barrier, len(friends) + sides + jnp.where(b == HUB, NB - 1, 1))
+
+    @pl.when(b == HUB)
+    def _():
+        for o in range(1, NB):
+            signal(ready, (zh * NB + (HUB + o) % NB, f))
+
     tell1()
 
     def transits(*pieces):
@@ -318,7 +333,7 @@
 
     hb = BLOCK // 2
 
-    def outer_send():
+    def outer_codes():
         in_g.wait()
         in_m.wait()
         drift = g[...].astype(F32) - w[rowof(x, j), :].astype(F32)
@@ -334,6 +349,12 @@
             oms[t] = jnp.concatenate(
                 [codes[yy][:, cut], codes[yy + 4][:, cut], scales[yy], scales[yy + 4]], axis=1
             )
+
+    def outer_send():
+        @pl.when(b != HUB)
+        def _():
+            pl.semaphore_wait(ready, 1)
+
         for o in range(1, NB):
             coa(o).start()
 
@@ -410,7 +431,7 @@
         ).astype(BF16)
         out_column(n, xx).start()
 
-    outer_send()
+    outer_codes()
     in_a[3].wait()
     xs[...] = partial_block(x)
     relay(7)
@@ -419,16 +440,17 @@
     relay(5)
     relay(4)
     transits(3, 2, 1, 0)
+    outer_send()
     hear1()
     tell2()
-    outer_sum()
     z_gather(2)
     settle(7)
     hear2(True)
     hear2(False)
     tell4()
+    outer_sum()
+    settle(6)
     outer_swap(1)
-    settle(6)
     z_gather(3)
     x_send(0)
     settle(5)
@@ -448,13 +470,13 @@
     z_gather(5)
     x_send(5)
     round2(4)
+    outer_swap(0)
     z_gather(6)
     x_send(6)
     settle(2)
     round1(2)
     settle(1)
     z_gather(7)
-    outer_swap(0)
     x_send(7)
     settle(0)
     x_relay(0)
@@ -579,6 +601,7 @@
             vmem((NB, ROWS, 128), BF16),
             dma((8,)),
             dma((8,)),
+            pltpu.SemaphoreType.REGULAR,
             pltpu.SemaphoreType.REGULAR((2,)),
             pltpu.SemaphoreType.REGULAR((2,)),
             pltpu.SemaphoreType.REGULAR,

time: 50.4 us -> 49.8 us (0.988)
  the two profiles are of different devices: /device:TPU:482 before, /device:TPU:1 now
where the time goes in v6:
time: 49.8 us; the launch traced here: 49.4 us
  Pallas kernels  47.7 us (96%)
  other arithmetic  1.06 us (2%)
  between operations  0.66 us (1%)
    pallas_call x1, Pallas kernels, per_device(): pl.pallas_call(kernel, name='joined_step', out_shape=shapes, in_specs=[hb...  46.5 us
    pallas_call x1, Pallas kernels, per_device(): pl.pallas_call(finish, name='finish', out_shape=shapes, in_specs=[hbm] *...  1.13 us
    concatenate x1, other arithmetic, per_device(): jnp.concatenate([kv_cotangent[0], local_weights[0], global_weights], axis=0)  1.06 us

profile of v6, /device:TPU:1, one launch (start us, length us, event | category | flops | bytes accessed | tf_op | source)
XLA Modules:
  0.0 49.4 jit_solution(15728068627816605325)
XLA Ops:
  0.6 0.0 copy-start
  0.6 1.1 %pad_maximum_fusion.b_hbm = bf16[384,512]{1,0:T(8,128)(2,1)S(1)} fusion(bf16[64,512]{1,0:T(8,128)(2,1)} %param.6, bf16[64,512]{1,0:T(8,128)(2,1)} %bitcast.10, bf16[256,512]{1,0:T(8,128)(2,1)} %bitcast.9), kind=kLoop, calls=%fused_computation | loop fusion | flops 1179648 | bytes 786432 | tf_op jit(solution)/shard_map/concatenate | solution.py:565
  1.7 0.0 copy-done
  1.7 46.5 %joined_step.1 = (bf16[256,512]{1,0:T(8,128)(2,1)S(1)}, bf16[256,2048]{1,0:T(8,128)(2,1)S(1)}, bf16[64,512]{1,0:T(8,128)(2,1)S(1)}, bf16[64,512]{1,0:T(8,128)(2,1)S(1)}, f32[32,64]{1,0:T(8,128)S(1)}) custom-call(f32[32,64]{1,0:T(8,128)S(1)} %bitcast.8, bf16[256,2048]{1,0:T(8,128)(2,1)} %bitcast.11, bf16[384,512]{1,0:T(8,128)(2,1)S(1)} %pad_maximum_fusion.b_hbm), custom_call_target="tpu_custom_call" | custom-call | flops 1610612736 | bytes 6291456 | tf_op jit(solution)/shard_map/joined_step/pallas_call | solution.py:566
  48.3 1.1 %finish.1 = (bf16[256,512]{1,0:T(8,128)(2,1)}, bf16[256,2048]{1,0:T(8,128)(2,1)}, bf16[64,512]{1,0:T(8,128)(2,1)}, bf16[64,512]{1,0:T(8,128)(2,1)}, f32[32,64]{1,0:T(8,128)}) custom-call(bf16[256,512]{1,0:T(8,128)(2,1)S(1)} %get-tuple-element.15.refs_0_, bf16[256,2048]{1,0:T(8,128)(2,1)S(1)} %get-tuple-element.16.refs_1_, ...), custom_call_target="tpu_custom_call" | custom-call | tf_op jit(solution)/shard_map/finish/pallas_call | solution.py:628
Async XLA Ops:
  0.6 1.1 %copy-start = (f32[64,32]{0,1:T(8,128)S(1)}, f32[64,32]{0,1:T(8,128)}, u32[]{:S(2)}) copy-start(f32[64,32]{0,1:T(8,128)} %param.7) | copy-start | bytes 24580

commit v7 on v6

--- a/solution.py
+++ b/solution.py
@@ -13,7 +13,7 @@
 NX = 4
 NZ = 8
 NB = 8
-HUB = 3
+HUB = 7
 ROWS = 64
 KV = 512
 D = 2048

time: 49.8 us -> 49.8 us (level)
  no operation moved by 1% of the time
where the time goes in v7:
time: 49.8 us; the launch traced here: 49.4 us
  Pallas kernels  47.7 us (96%)
  other arithmetic  1.06 us (2%)
  between operations  0.66 us (1%)
    pallas_call x1, Pallas kernels, per_device(): pl.pallas_call(kernel, name='joined_step', out_shape=shapes, in_specs=[hb...  46.5 us
    pallas_call x1, Pallas kernels, per_device(): pl.pallas_call(finish, name='finish', out_shape=shapes, in_specs=[hbm] *...  1.13 us
    concatenate x1, other arithmetic, per_device(): jnp.concatenate([kv_cotangent[0], local_weights[0], global_weights], axis=0)  1.06 us

profile of v7, /device:TPU:1, one launch (start us, length us, event | category | flops | bytes accessed | tf_op | source)
XLA Modules:
  0.0 49.4 jit_solution(6222056307650295717)
XLA Ops:
  0.6 0.0 copy-start
  0.6 1.1 %pad_maximum_fusion.b_hbm = bf16[384,512]{1,0:T(8,128)(2,1)S(1)} fusion(bf16[64,512]{1,0:T(8,128)(2,1)} %param.6, bf16[64,512]{1,0:T(8,128)(2,1)} %bitcast.10, bf16[256,512]{1,0:T(8,128)(2,1)} %bitcast.9), kind=kLoop, calls=%fused_computation | loop fusion | flops 1179648 | bytes 786432 | tf_op jit(solution)/shard_map/concatenate | solution.py:565
  1.7 0.0 copy-done
  1.7 46.5 %joined_step.1 = (bf16[256,512]{1,0:T(8,128)(2,1)S(1)}, bf16[256,2048]{1,0:T(8,128)(2,1)S(1)}, bf16[64,512]{1,0:T(8,128)(2,1)S(1)}, bf16[64,512]{1,0:T(8,128)(2,1)S(1)}, f32[32,64]{1,0:T(8,128)S(1)}) custom-call(f32[32,64]{1,0:T(8,128)S(1)} %bitcast.8, bf16[256,2048]{1,0:T(8,128)(2,1)} %bitcast.11, bf16[384,512]{1,0:T(8,128)(2,1)S(1)} %pad_maximum_fusion.b_hbm), custom_call_target="tpu_custom_call" | custom-call | flops 1610612736 | bytes 6291456 | tf_op jit(solution)/shard_map/joined_step/pallas_call | solution.py:566
  48.3 1.1 %finish.1 = (bf16[256,512]{1,0:T(8,128)(2,1)}, bf16[256,2048]{1,0:T(8,128)(2,1)}, bf16[64,512]{1,0:T(8,128)(2,1)}, bf16[64,512]{1,0:T(8,128)(2,1)}, f32[32,64]{1,0:T(8,128)}) custom-call(bf16[256,512]{1,0:T(8,128)(2,1)S(1)} %get-tuple-element.15.refs_0_, bf16[256,2048]{1,0:T(8,128)(2,1)S(1)} %get-tuple-element.16.refs_1_, ...), custom_call_target="tpu_custom_call" | custom-call | tf_op jit(solution)/shard_map/finish/pallas_call | solution.py:628
Async XLA Ops:
  0.6 1.1 %copy-start = (f32[64,32]{0,1:T(8,128)S(1)}, f32[64,32]{0,1:T(8,128)}, u32[]{:S(2)}) copy-start(f32[64,32]{0,1:T(8,128)} %param.7) | copy-start | bytes 24580
